TPU v7x, 32 devices: a whole 2x2x4 slice. The times are simulated.
32 devices in a mesh: section: 16 (over z, y, x), attn: 2 (over core).
Axes of the slice: x: 2, y: 2, z: 4, core: 2. Of those that a mesh axis runs over, the one named last changes fastest.
Arguments:
- queries: bfloat16 [8192, 3072], P(('section', 'attn')), may hold values from -120 to 120
- keys: bfloat16 [8192, 1024], P(('section', 'attn')), may hold values from -2.5 to 2.5
- values: bfloat16 [8192, 1024], P(('section', 'attn')), may hold values from -4 to 4
- doc_ids: int32 [8192], replicated, may hold values from 0 to 15, never falling along the last dimension, each value on 1 to 1792 neighbouring positions
Outputs:
- attended: bfloat16 [8192, 3072], P(('section', 'attn'))
Inputs may be any that keep to these rules, and one draw needn't show every extreme that they name: `doc_ids`: along the pack the document numbers never fall, and a document holds at most 1792 tokens.
All inputs are finite; a program needn't handle non-finite values.
Results may differ from a plain program's by a relative error of at most 0.0028.
Values may be sent and summed in bfloat16 or wider, within the bound.
No kernel may reach another device: no remote copies, remote signals or barrier semaphores. Data moves between devices by JAX's collectives and lax.ppermute only.
A program may use at most 64 MiB of HBM per device.

v0:
```python
import functools
import math

import jax
import jax.numpy as jnp
from jax import lax
from jax.experimental import pallas as pl
from jax.experimental.pallas import tpu as pltpu
from jax.sharding import PartitionSpec as P

HEAD_DIM = 128
REACH = 8
AXES = ("section", "attn")
NEG = -1e30
SCALE = HEAD_DIM ** -0.5 * math.log2(math.e)
HEADS_STEP = 2
HIGH = 60.0
barrier = lax.optimization_barrier


def scores(q, k, allowed):
    s = lax.dot_general(q, k, (((1,), (1,)), ((), ())), preferred_element_type=jnp.float32)
    return jnp.where(allowed, s, NEG)


def weigh(w, v):
    total = jnp.sum(w, axis=1, keepdims=True)
    return total, jnp.dot(w.astype(jnp.bfloat16), v, preferred_element_type=jnp.float32)


def read_stats(ref, head):
    return ref[:, 2 * head:2 * head + 1], ref[:, 2 * head + 1:2 * head + 2]


def write_stats(ref, pairs):
    lane = lax.broadcasted_iota(jnp.int32, ref.shape, 1)
    tile = jnp.zeros(ref.shape, jnp.float32)
    for head, (top, total) in enumerate(pairs):
        tile = jnp.where(lane == 2 * head, top, jnp.where(lane == 2 * head + 1, total, tile))
    ref[...] = tile


def cut(ref, h, width=HEAD_DIM):
    return ref[:, h * width:(h + 1) * width]


def own_kernel(group, info, q_ref, start_ref, k_ref, v_ref, mk_ref, mv_ref, acc_ref, stat_ref):
    rows = q_ref.shape[0]
    start = start_ref[...]
    at = lax.broadcasted_iota(jnp.int32, (rows, rows), 1)
    row = lax.broadcasted_iota(jnp.int32, (rows, rows), 0)
    own_ok = (at <= row) & (at + info[0] >= start)
    mate_ok = at + info[1] >= start
    allowed = jnp.concatenate([own_ok, mate_ok], axis=1)
    pairs = []
    for h in range(HEADS_STEP):
        k = jnp.concatenate([cut(k_ref, h), cut(mk_ref, h)], axis=0)
        v = jnp.concatenate([cut(v_ref, h), cut(mv_ref, h)], axis=0)
        for head in range(h * group, (h + 1) * group):
            s = scores(cut(q_ref, head), k, allowed)
            top = jnp.max(s, axis=1, keepdims=True)
            total, out = weigh(jnp.exp2((s - top) * SCALE), v)
            acc_ref[:, head * HEAD_DIM:(head + 1) * HEAD_DIM] = out
            pairs.append((top, total))
    write_stats(stat_ref, pairs)


def far_kernel(group, choose, last, info, q_ref, start_ref, acc_in, stat_in, *refs):
    rows = q_ref.shape[0]
    pieces, outs = (refs[:-1], refs[-1:]) if last else (refs[:-2], refs[-2:])
    heads = HEADS_STEP * group
    needed = info[1] > 0

    def put(head, total, out):
        if last:
            out = (out / total).astype(jnp.bfloat16)
        outs[0][:, head * HEAD_DIM:(head + 1) * HEAD_DIM] = out

    def attend(exact):
        start = start_ref[...]
        at = lax.broadcasted_iota(jnp.int32, (rows, rows), 1)
        allowed = jnp.concatenate([at + info[2 + i] >= start for i in range(4)], axis=1)
        pairs, high = [], None
        for h in range(HEADS_STEP):
            ks, vs = choose(info[0], [cut(r, h) for r in pieces])
            k, v = jnp.concatenate(ks, axis=0), jnp.concatenate(vs, axis=0)
            for head in range(h * group, (h + 1) * group):
                s = scores(cut(q_ref, head), k, allowed)
                top, total = read_stats(stat_in, head)
                before = cut(acc_in, head)
                if exact:
                    new = jnp.maximum(top, jnp.max(s, axis=1, keepdims=True))
                    back = jnp.exp2((top - new) * SCALE)
                    top, total, before = new, total * back, before * back
                power = (s - top) * SCALE
                if not exact:
                    peak = jnp.max(power.reshape(rows // 8, 8, -1, HEAD_DIM), axis=(0, 2))
                    high = peak if high is None else jnp.maximum(high, peak)
                more, out = weigh(jnp.exp2(power), v)
                total = total + more
                put(head, total, out + before)
                pairs.append((top, total))
        if not last:
            write_stats(outs[1], pairs)
        return high

    @pl.when(needed)
    def _():
        high = attend(False)

        @pl.when(jnp.max(high) > HIGH)
        def _():
            attend(True)

    @pl.when(jnp.logical_not(needed))
    def _():
        for head in range(heads):
            put(head, read_stats(stat_in, head)[1], cut(acc_in, head))
        if not last:
            outs[1][...] = stat_in[...]


def pick(plane, at0, at1, at2, at3):
    return jnp.where(plane == 0, at0, jnp.where(plane == 1, at1, jnp.where(plane == 2, at2, at3)))


def choose_middle(plane, tiles):
    def half(x1, y1, z1, x2, y2, z2, odd_k, odd_v):
        pk, pv = pick(plane, x2, x2, y2, x2), pick(plane, z2, x1, y1, x1)
        qk, qv = pick(plane, odd_k, y2, x2, y2), pick(plane, odd_v, z2, z2, y1)
        return pk, pv, qk, qv
    near, far = tiles[:6], tiles[6:]
    a, b = half(*near, far[2], near[2]), half(*far, far[2], near[2])
    return (a[0], b[0], a[2], b[2]), (a[1], b[1], a[3], b[3])


def choose_last(plane, tiles):
    def half(z1, y2, x3, y3, z3):
        pk, pv = pick(plane, y2, x3, x3, x3), pick(plane, z3, y3, y3, y3)
        qk, qv = pick(plane, x3, z1, z1, z1), pick(plane, y3, z3, z3, z3)
        return pk, pv, qk, qv
    a, b = half(*tiles[:5]), half(*tiles[5:])
    return (a[0], b[0], a[2], b[2]), (a[1], b[1], a[3], b[3])


def call(kernel, info, q, start, carry, pieces, last, keys):
    rows, width = q.shape
    heads = pieces[0].shape[1] // HEAD_DIM
    group = width // pieces[0].shape[1]
    step = HEADS_STEP * HEAD_DIM

    def block(columns):
        return pl.BlockSpec((rows, columns), lambda j, *_: (0, j))

    wide, narrow, stats = block(group * step), block(step), block(HEAD_DIM)
    out_shape = [jax.ShapeDtypeStruct(q.shape, jnp.bfloat16 if last else jnp.float32)]
    out_specs = [wide]
    if not last:
        out_shape.append(jax.ShapeDtypeStruct((rows, heads // HEADS_STEP * HEAD_DIM), jnp.float32))
        out_specs.append(stats)
    return pl.pallas_call(
        functools.partial(kernel, group),
        grid_spec=pltpu.PrefetchScalarGridSpec(
            num_scalar_prefetch=1,
            grid=(heads // HEADS_STEP,),
            in_specs=[wide, pl.BlockSpec((rows, 1), lambda j, *_: (0, 0))]
            + [wide, stats][:len(carry)] + [narrow] * len(pieces),
            out_specs=out_specs,
        ),
        out_shape=out_shape,
        cost_estimate=pl.CostEstimate(
            flops=8 * rows * keys * width, bytes_accessed=4 * rows * width, transcendentals=0
        ),
        compiler_params=pltpu.CompilerParams(vmem_limit_bytes=40 * 2**20),
    )(info, q, start, *carry, *pieces)


def shards(queries, keys, values, doc_ids):
    rows = queries.shape[0]
    chips, cores = lax.axis_size("section"), lax.axis_size("attn")
    chip, core = lax.axis_index("section"), lax.axis_index("attn")
    owner = chip * cores + core
    plane, odd_x, odd_y = chip % 4, chip % 2, (chip // 2) % 2

    def routes(target):
        return [(c * cores + k, target(c) * cores + k) for c in range(chips) for k in range(cores)]

    along = {"x": routes(lambda c: c ^ 1), "y": routes(lambda c: c ^ 2), "z": routes(lambda c: (c + 4) % chips)}
    along["mate"] = [(c * cores + k, c * cores + 1 - k) for c in range(chips) for k in range(cores)]

    def send(array, way):
        return lax.ppermute(array, AXES, along[way])

    def swap(*arrays):
        return tuple(send(a, "mate") for a in arrays)

    first = owner * rows
    span = min(REACH * rows, doc_ids.shape[0])
    low = jnp.maximum(first - (REACH - 1) * rows, 0)
    window = lax.dynamic_slice_in_dim(doc_ids, low, span)
    query_doc = lax.dynamic_slice_in_dim(doc_ids, first, rows)
    start = low + jnp.sum((window[None, :] < query_doc[:, None]).astype(jnp.int32), axis=1, keepdims=True)
    none = jnp.int32(-(2**30))

    def place(device, ok=True):
        return jnp.where((device >= 0) & (device < owner) & ok, device * rows, none)

    def info_of(places):
        newest = functools.reduce(jnp.maximum, places)
        needed = (newest + rows > start[0, 0]).astype(jnp.int32)
        return jnp.stack([plane, needed] + places)

    def halves(back):
        base = (chip - back) * cores
        return [place(base + core), place(base + 1 - core)]

    own_info = jnp.stack([first, place(owner - 1, core == 1)])
    extra = place(chip * cores - 7, core == 0)
    q_places = halves(pick(plane, 0, 2, 3, 2))
    q_places = [jnp.where(plane == 0, extra, q_places[0]), jnp.where(plane == 0, none, q_places[1])]
    middle_info = info_of(halves(pick(plane, 3, 1, 2, 1)) + q_places)
    last_info = info_of(halves(pick(plane, 2, 3, 1, 3)) + halves(pick(plane, 1, 4, 4, 4)))

    w = jnp.where
    mate_k, mate_v = swap(keys, values)
    x1, y1 = send(values, "x"), send(values, "y")
    z1 = send(w((plane == 0) & (core == 0), mate_v, keys), "z")
    acc, stat = call(own_kernel, own_info, queries, start, (), [keys, values, mate_k, mate_v], False, 2 * rows)
    x1, y1, z1, acc, stat, middle_info, last_info = barrier((x1, y1, z1, acc, stat, middle_info, last_info))
    x2 = send(w(odd_x == 0, keys, z1), "x")
    y2 = send(w(odd_y == 0, keys, z1), "y")
    z2 = send(w(plane == 1, y1, x1), "z")
    x1s, y1s, z1s = swap(x1, y1, z1)
    x2, y2, z2 = barrier((x2, y2, z2))
    x3 = send(y2, "x")
    y3 = send(w(odd_y == 0, x1, z2), "y")
    z3 = send(w(plane == 0, y1, values), "z")
    x2s, y2s, z2s = swap(x2, y2, z2)
    acc, stat = call(
        lambda group, *refs: far_kernel(group, choose_middle, False, *refs),
        middle_info, queries, start, (acc, stat),
        [x1, y1, z1, x2, y2, z2, x1s, y1s, z1s, x2s, y2s, z2s], False, 4 * rows,
    )
    x3, y3, z3, acc, stat = barrier((x3, y3, z3, acc, stat))
    x3s, y3s, z3s = swap(x3, y3, z3)
    (out,) = call(
        lambda group, *refs: far_kernel(group, choose_last, True, *refs),
        last_info, queries, start, (acc, stat),
        [z1, y2, x3, y3, z3, z1s, y2s, x3s, y3s, z3s], True, 4 * rows,
    )
    return out


def solution(mesh):
    split = P(AXES, None)
    return jax.shard_map(
        shards, mesh=mesh, in_specs=(split, split, split, P()), out_specs=split, check_vma=False
    )
```

profile of v0, /device:TPU:13, one launch (start us, length us, event | category | flops | bytes accessed | tf_op | source)
XLA Modules:
  0.0 85.6 jit_solution(6343970319386784352)
XLA Ops:
  0.0 0.7 collective-permute-start.2
  0.7 1.2 %collective-permute-start = (bf16[256,1024]{1,0:T(8,128)(2,1)}, bf16[256,1024]{1,0:T(8,128)(2,1)S(1)}, u32[]{:S(2)}, u32[]{:S(2)}) collective-permute-start(bf16[256,1024]{1,0:T(8,128)(2,1)} %v_ref.1), channel_id=1, source_target_pairs={{0,2},{1,3},{2,0},{3,1},{4,6},{5,7},{6,4},{7,5},{8,10},{9,11},{10,... | collective-permute-start | bytes 1572872 | tf_op jit(solution)/shard_map/ppermute | solution.py:192
  1.9 0.2 collective-permute-start.1
  2.1 0.6 collective-permute-start.4
  2.7 0.8 dynamic_slice.7
  3.4 0.8 dynamic_slice.6
  4.2 0.4 convert_reduce_fusion
  4.6 0.0 collective-permute-done.2.mv_ref
  4.6 1.1 %broadcast_select_fusion.5 = bf16[256,1024]{1,0:T(8,128)(2,1)S(1)} fusion(bf16[256,1024]{1,0:T(8,128)(2,1)S(1)} %collective-permute-done.2.mv_ref, bf16[256,1024]{1,0:T(8,128)(2,1)} %k_ref.1, pred[]{:T(512)S(6)} %and.60), kind=kLoop, calls=%fused_computation.6 | loop fusion | flops 262144 | bytes 1572865 | tf_op jit(solution)/shard_map/jit(_where)/select_n | solution.py:227
  5.7 1.3 %collective-permute-start.3 = (bf16[256,1024]{1,0:T(8,128)(2,1)S(1)}, bf16[256,1024]{1,0:T(8,128)(2,1)S(1)}, u32[]{:S(2)}, u32[]{:S(2)}) collective-permute-start(bf16[256,1024]{1,0:T(8,128)(2,1)S(1)} %broadcast_select_fusion.5), channel_id=1, source_target_pairs={{0,8},{1,9},{2,10},{3,11},{4,12},{5,13},{6,14},{7,15},{8,16},{9,17... | collective-permute-start | bytes 1572872 | tf_op jit(solution)/shard_map/ppermute | solution.py:192
  7.0 0.5 slice.5
  8.1 0.1 copy.8.start_ref.refs_2_
  8.9 0.1 stack.65.refs_0_
  9.0 0.1 stack.72.refs_0_
  9.1 0.1 pad_add_fusion.info
  9.1 0.0 collective-permute-done.4.mk_ref
  9.1 0.0 copy-start
  9.2 1.0 %copy-done = bf16[256,1024]{1,0:T(8,128)(2,1)S(1)} copy-done((bf16[256,1024]{1,0:T(8,128)(2,1)S(1)}, bf16[256,1024]{1,0:T(8,128)(2,1)}, u32[]{:S(2)}) %copy-start) | copy-done | bytes 524312
  10.2 0.0 copy-start.1
  10.2 1.0 %copy-done.1 = bf16[256,1024]{1,0:T(8,128)(2,1)S(1)} copy-done((bf16[256,1024]{1,0:T(8,128)(2,1)S(1)}, bf16[256,1024]{1,0:T(8,128)(2,1)}, u32[]{:S(2)}) %copy-start.1) | copy-done | bytes 524312
  11.2 0.0 copy-start.2
  11.2 1.4 %copy-done.2 = bf16[256,3072]{1,0:T(8,128)(2,1)S(1)} copy-done((bf16[256,3072]{1,0:T(8,128)(2,1)S(1)}, bf16[256,3072]{1,0:T(8,128)(2,1)}, u32[]{:S(2)}) %copy-start.2) | copy-done | bytes 1572888
  12.6 9.4 %shard_map.46 = (f32[256,3072]{1,0:T(8,128)S(1)}, f32[256,512]{1,0:T(8,128)S(1)}) custom-call(s32[2]{0:T(128)S(1)} %pad_add_fusion.info, bf16[256,3072]{1,0:T(8,128)(2,1)S(1)} %copy-done.2, s32[256,1]{1,0:T(8,128)S(1)} %copy.8.start_ref.refs_2_, bf16[256,1024]{1,0:T(8,128)(2,1)S(1)} %copy-done, bf16[256,1024]{1,0:T(8,128)(2,1)S(1)} %copy-done.1, ...), custom_call_target="tpu_custom_call" | custom-call | flops 3221225472 | bytes 3145728 | tf_op jit(solution)/shard_map/pallas_call | solution.py:161
  22.1 0.0 copy-start.3
  22.1 0.0 collective-permute-done.refs_5_
  22.1 0.0 collective-permute-done.1.refs_6_
  22.1 0.0 collective-permute-done.3.refs_7_.refs_5_
  22.1 0.1 broadcast_select_fusion
  22.2 1.4 %collective-permute-start.7 = (bf16[256,1024]{1,0:T(8,128)(2,1)S(1)}, bf16[256,1024]{1,0:T(8,128)(2,1)S(1)}, u32[]{:S(2)}, u32[]{:S(2)}) collective-permute-start(bf16[256,1024]{1,0:T(8,128)(2,1)S(1)} %get-tuple-element.46), channel_id=1, source_target_pairs={{0,8},{1,9},{2,10},{3,11},{4,12},{5,13},{6,14},{7,15},{8,16},{9,17... | collective-permute-start | bytes 1572872 | tf_op jit(solution)/shard_map/ppermute | solution.py:192
  23.6 0.1 broadcast_select_fusion.3
  23.7 0.1 copy-done.3
  23.7 0.3 collective-permute-start.5
  24.0 1.2 %collective-permute-start.6 = (bf16[256,1024]{1,0:T(8,128)(2,1)S(1)}, bf16[256,1024]{1,0:T(8,128)(2,1)S(1)}, u32[]{:S(2)}, u32[]{:S(2)}) collective-permute-start(bf16[256,1024]{1,0:T(8,128)(2,1)S(1)} %get-tuple-element.43), channel_id=1, source_target_pairs={{0,4},{1,5},{2,6},{3,7},{4,0},{5,1},{6,2},{7,3},{8,12},{9,13},{10,... | collective-permute-start | bytes 1572872 | tf_op jit(solution)/shard_map/ppermute | solution.py:192
  25.2 1.1 %collective-permute-start.11 = (bf16[256,1024]{1,0:T(8,128)(2,1)S(1)}, bf16[256,1024]{1,0:T(8,128)(2,1)S(1)}, u32[]{:S(2)}, u32[]{:S(2)}) collective-permute-start(bf16[256,1024]{1,0:T(8,128)(2,1)S(1)} %collective-permute-done.refs_5_), channel_id=1, source_target_pairs={{0,1},{1,0},{2,3},{3,2},{4,5},{5,4},{6,7},{7,6},{8,9},{9,8},{10,11... | collective-permute-start | bytes 1572872 | tf_op jit(solution)/shard_map/ppermute | solution.py:192
  26.4 0.0 collective-permute-start.12
  26.4 9.2 %collective-permute-done.7.refs_10_ = bf16[256,1024]{1,0:T(8,128)(2,1)S(1)} collective-permute-done((bf16[256,1024]{1,0:T(8,128)(2,1)S(1)}, bf16[256,1024]{1,0:T(8,128)(2,1)S(1)}, u32[]{:S(2)}, u32[]{:S(2)}) %collective-permute-start.7) | collective-permute-done | bytes 524320 | tf_op jit(solution)/shard_map/ppermute | solution.py:192
  35.5 1.1 %collective-permute-start.13 = (bf16[256,1024]{1,0:T(8,128)(2,1)S(1)}, bf16[256,1024]{1,0:T(8,128)(2,1)S(1)}, u32[]{:S(2)}, u32[]{:S(2)}) collective-permute-start(bf16[256,1024]{1,0:T(8,128)(2,1)S(1)} %collective-permute-done.3.refs_7_.refs_5_), channel_id=1, source_target_pairs={{0,1},{1,0},{2,3},{3,2},{4,5},{5,4},{6,7},{7,6},{8,9},{9,8},{10,11... | collective-permute-start | bytes 1572872 | tf_op jit(solution)/shard_map/ppermute | solution.py:192
  36.6 0.0 collective-permute-done.5.refs_8_
  36.7 0.0 collective-permute-done.6.refs_9_.refs_6_
  36.7 1.7 %collective-permute-start.14 = (bf16[256,1024]{1,0:T(8,128)(2,1)S(1)}, bf16[256,1024]{1,0:T(8,128)(2,1)S(1)}, u32[]{:S(2)}, u32[]{:S(2)}) collective-permute-start(bf16[256,1024]{1,0:T(8,128)(2,1)S(1)} %collective-permute-done.5.refs_8_), channel_id=1, source_target_pairs={{0,1},{1,0},{2,3},{3,2},{4,5},{5,4},{6,7},{7,6},{8,9},{9,8},{10,11... | collective-permute-start | bytes 1572872 | tf_op jit(solution)/shard_map/ppermute | solution.py:192
  38.3 0.0 collective-permute-start.15
  38.3 0.0 collective-permute-done.11.refs_11_
  38.3 0.5 collective-permute-start.16
  38.8 0.1 broadcast_select_fusion.2
  38.9 0.0 collective-permute-done.12.refs_12_
  38.9 1.5 %collective-permute-start.10 = (bf16[256,1024]{1,0:T(8,128)(2,1)S(1)}, bf16[256,1024]{1,0:T(8,128)(2,1)S(1)}, u32[]{:S(2)}, u32[]{:S(2)}) collective-permute-start(bf16[256,1024]{1,0:T(8,128)(2,1)S(1)} %get-tuple-element.45), channel_id=1, source_target_pairs={{0,8},{1,9},{2,10},{3,11},{4,12},{5,13},{6,14},{7,15},{8,16},{9,17... | collective-permute-start | bytes 1572872 | tf_op jit(solution)/shard_map/ppermute | solution.py:192
  40.4 0.0 collective-permute-done.13.refs_13_.refs_10_
  40.4 1.2 %collective-permute-start.8 = (bf16[256,1024]{1,0:T(8,128)(2,1)S(1)}, bf16[256,1024]{1,0:T(8,128)(2,1)S(1)}, u32[]{:S(2)}, u32[]{:S(2)}) collective-permute-start(bf16[256,1024]{1,0:T(8,128)(2,1)S(1)} %collective-permute-done.6.refs_9_.refs_6_), channel_id=1, source_target_pairs={{0,2},{1,3},{2,0},{3,1},{4,6},{5,7},{6,4},{7,5},{8,10},{9,11},{10,... | collective-permute-start | bytes 1572872 | tf_op jit(solution)/shard_map/ppermute | solution.py:192
  41.7 0.0 collective-permute-done.14.refs_14_
  41.7 1.2 %collective-permute-start.9 = (bf16[256,1024]{1,0:T(8,128)(2,1)S(1)}, bf16[256,1024]{1,0:T(8,128)(2,1)S(1)}, u32[]{:S(2)}, u32[]{:S(2)}) collective-permute-start(bf16[256,1024]{1,0:T(8,128)(2,1)S(1)} %broadcast_select_fusion.2), channel_id=1, source_target_pairs={{0,4},{1,5},{2,6},{3,7},{4,0},{5,1},{6,2},{7,3},{8,12},{9,13},{10,... | collective-permute-start | bytes 1572872 | tf_op jit(solution)/shard_map/ppermute | solution.py:192
  42.9 0.0 collective-permute-done.15.refs_15_.refs_11_
  42.9 0.0 collective-permute-done.16.refs_16_
  42.9 19.4 %shard_map.47 = (f32[256,3072]{1,0:T(8,128)S(1)}, f32[256,512]{1,0:T(8,128)S(1)}) custom-call(s32[6]{0:T(128)S(1)} %stack.65.refs_0_, bf16[256,3072]{1,0:T(8,128)(2,1)S(1)} %copy-done.2, s32[256,1]{1,0:T(8,128)S(1)} %copy.8.start_ref.refs_2_, f32[256,3072]{1,0:T(8,128)} %copy-done.3, f32[256,512]{1,0:T(8,128)S(1)} %get-tuple-element.34.refs_4_, ...), custom_call_target="tpu_custom_call" | custom-call | flops 6442450944 | bytes 3145728 | tf_op jit(solution)/shard_map/pallas_call | solution.py:161
  62.3 0.0 collective-permute-done.10.refs_9_
  62.3 0.0 collective-permute-done.9.refs_8_
  62.3 0.0 collective-permute-done.8.refs_7_
  62.3 1.1 %collective-permute-start.17 = (bf16[256,1024]{1,0:T(8,128)(2,1)S(1)}, bf16[256,1024]{1,0:T(8,128)(2,1)S(1)}, u32[]{:S(2)}, u32[]{:S(2)}) collective-permute-start(bf16[256,1024]{1,0:T(8,128)(2,1)S(1)} %collective-permute-done.8.refs_7_), channel_id=1, source_target_pairs={{0,1},{1,0},{2,3},{3,2},{4,5},{5,4},{6,7},{7,6},{8,9},{9,8},{10,11... | collective-permute-start | bytes 1572872 | tf_op jit(solution)/shard_map/ppermute | solution.py:192
  63.4 0.1 collective-permute-start.18
  63.4 0.4 collective-permute-start.19
  63.9 1.0 %collective-permute-done.17.refs_12_ = bf16[256,1024]{1,0:T(8,128)(2,1)S(1)} collective-permute-done((bf16[256,1024]{1,0:T(8,128)(2,1)S(1)}, bf16[256,1024]{1,0:T(8,128)(2,1)S(1)}, u32[]{:S(2)}, u32[]{:S(2)}) %collective-permute-start.17) | collective-permute-done | bytes 524320 | tf_op jit(solution)/shard_map/ppermute | solution.py:192
  64.9 0.7 collective-permute-done.18.refs_13_
  65.7 0.7 collective-permute-done.19.refs_14_
  66.4 19.2 %shard_map.48 = bf16[256,3072]{1,0:T(8,128)(2,1)} custom-call(s32[6]{0:T(128)S(1)} %stack.72.refs_0_, bf16[256,3072]{1,0:T(8,128)(2,1)S(1)} %copy-done.2, s32[256,1]{1,0:T(8,128)S(1)} %copy.8.start_ref.refs_2_, f32[256,3072]{1,0:T(8,128)S(1)} %get-tuple-element.38.refs_3_, f32[256,512]{1,0:T(8,128)S(1)} %get-tuple-element.39.refs_4_, ...), custom_call_target="tpu_custom_call" | custom-call | flops 6442450944 | bytes 3145728 | tf_op jit(solution)/shard_map/pallas_call | solution.py:161
  (1 shorter events, 0.0 us)
Async XLA Ops:
  0.0 4.6 %collective-permute-start.2 = (bf16[256,1024]{1,0:T(8,128)(2,1)}, bf16[256,1024]{1,0:T(8,128)(2,1)S(1)}, u32[]{:S(2)}, u32[]{:S(2)}) collective-permute-start(bf16[256,1024]{1,0:T(8,128)(2,1)} %v_ref.1), channel_id=1, source_target_pairs={{0,1},{1,0},{2,3},{3,2},{4,5},{5,4},{6,7},{7,6},{8,9},{9,8},{10,11... | collective-permute-start | bytes 1572872 | tf_op jit(solution)/shard_map/ppermute | solution.py:192
  0.7 21.4 %collective-permute-start = (bf16[256,1024]{1,0:T(8,128)(2,1)}, bf16[256,1024]{1,0:T(8,128)(2,1)S(1)}, u32[]{:S(2)}, u32[]{:S(2)}) collective-permute-start(bf16[256,1024]{1,0:T(8,128)(2,1)} %v_ref.1), channel_id=1, source_target_pairs={{0,2},{1,3},{2,0},{3,1},{4,6},{5,7},{6,4},{7,5},{8,10},{9,11},{10,... | collective-permute-start | bytes 1572872 | tf_op jit(solution)/shard_map/ppermute | solution.py:192
  1.9 20.2 %collective-permute-start.1 = (bf16[256,1024]{1,0:T(8,128)(2,1)}, bf16[256,1024]{1,0:T(8,128)(2,1)S(1)}, u32[]{:S(2)}, u32[]{:S(2)}) collective-permute-start(bf16[256,1024]{1,0:T(8,128)(2,1)} %v_ref.1), channel_id=1, source_target_pairs={{0,4},{1,5},{2,6},{3,7},{4,0},{5,1},{6,2},{7,3},{8,12},{9,13},{10,... | collective-permute-start | bytes 1572872 | tf_op jit(solution)/shard_map/ppermute | solution.py:192
  2.1 7.0 %collective-permute-start.4 = (bf16[256,1024]{1,0:T(8,128)(2,1)}, bf16[256,1024]{1,0:T(8,128)(2,1)S(1)}, u32[]{:S(2)}, u32[]{:S(2)}) collective-permute-start(bf16[256,1024]{1,0:T(8,128)(2,1)} %k_ref.1), channel_id=1, source_target_pairs={{0,1},{1,0},{2,3},{3,2},{4,5},{5,4},{6,7},{7,6},{8,9},{9,8},{10,11... | collective-permute-start | bytes 1572872 | tf_op jit(solution)/shard_map/ppermute | solution.py:192
  5.7 16.4 %collective-permute-start.3 = (bf16[256,1024]{1,0:T(8,128)(2,1)S(1)}, bf16[256,1024]{1,0:T(8,128)(2,1)S(1)}, u32[]{:S(2)}, u32[]{:S(2)}) collective-permute-start(bf16[256,1024]{1,0:T(8,128)(2,1)S(1)} %broadcast_select_fusion.5), channel_id=1, source_target_pairs={{0,8},{1,9},{2,10},{3,11},{4,12},{5,13},{6,14},{7,15},{8,16},{9,17... | collective-permute-start | bytes 1572872 | tf_op jit(solution)/shard_map/ppermute | solution.py:192
  9.1 1.0 %copy-start = (bf16[256,1024]{1,0:T(8,128)(2,1)S(1)}, bf16[256,1024]{1,0:T(8,128)(2,1)}, u32[]{:S(2)}) copy-start(bf16[256,1024]{1,0:T(8,128)(2,1)} %k_ref.1) | copy-start | bytes 1572868
  10.2 1.0 %copy-start.1 = (bf16[256,1024]{1,0:T(8,128)(2,1)S(1)}, bf16[256,1024]{1,0:T(8,128)(2,1)}, u32[]{:S(2)}) copy-start(bf16[256,1024]{1,0:T(8,128)(2,1)} %v_ref.1) | copy-start | bytes 1572868
  11.2 1.4 %copy-start.2 = (bf16[256,3072]{1,0:T(8,128)(2,1)S(1)}, bf16[256,3072]{1,0:T(8,128)(2,1)}, u32[]{:S(2)}) copy-start(bf16[256,3072]{1,0:T(8,128)(2,1)} %refs_1_.3) | copy-start | bytes 4718596
  22.1 1.6 %copy-start.3 = (f32[256,3072]{1,0:T(8,128)}, f32[256,3072]{1,0:T(8,128)S(1)}, u32[]{:S(2)}) copy-start(f32[256,3072]{1,0:T(8,128)S(1)} %get-tuple-element.33.refs_3_) | copy-start | bytes 9437188
  22.2 13.3 %collective-permute-start.7 = (bf16[256,1024]{1,0:T(8,128)(2,1)S(1)}, bf16[256,1024]{1,0:T(8,128)(2,1)S(1)}, u32[]{:S(2)}, u32[]{:S(2)}) collective-permute-start(bf16[256,1024]{1,0:T(8,128)(2,1)S(1)} %get-tuple-element.46), channel_id=1, source_target_pairs={{0,8},{1,9},{2,10},{3,11},{4,12},{5,13},{6,14},{7,15},{8,16},{9,17... | collective-permute-start | bytes 1572872 | tf_op jit(solution)/shard_map/ppermute | solution.py:192
  23.7 12.9 %collective-permute-start.5 = (bf16[256,1024]{1,0:T(8,128)(2,1)S(1)}, bf16[256,1024]{1,0:T(8,128)(2,1)S(1)}, u32[]{:S(2)}, u32[]{:S(2)}) collective-permute-start(bf16[256,1024]{1,0:T(8,128)(2,1)S(1)} %get-tuple-element.44), channel_id=1, source_target_pairs={{0,2},{1,3},{2,0},{3,1},{4,6},{5,7},{6,4},{7,5},{8,10},{9,11},{10,... | collective-permute-start | bytes 1572872 | tf_op jit(solution)/shard_map/ppermute | solution.py:192
  24.0 12.7 %collective-permute-start.6 = (bf16[256,1024]{1,0:T(8,128)(2,1)S(1)}, bf16[256,1024]{1,0:T(8,128)(2,1)S(1)}, u32[]{:S(2)}, u32[]{:S(2)}) collective-permute-start(bf16[256,1024]{1,0:T(8,128)(2,1)S(1)} %get-tuple-element.43), channel_id=1, source_target_pairs={{0,4},{1,5},{2,6},{3,7},{4,0},{5,1},{6,2},{7,3},{8,12},{9,13},{10,... | collective-permute-start | bytes 1572872 | tf_op jit(solution)/shard_map/ppermute | solution.py:192
  25.2 13.1 %collective-permute-start.11 = (bf16[256,1024]{1,0:T(8,128)(2,1)S(1)}, bf16[256,1024]{1,0:T(8,128)(2,1)S(1)}, u32[]{:S(2)}, u32[]{:S(2)}) collective-permute-start(bf16[256,1024]{1,0:T(8,128)(2,1)S(1)} %collective-permute-done.refs_5_), channel_id=1, source_target_pairs={{0,1},{1,0},{2,3},{3,2},{4,5},{5,4},{6,7},{7,6},{8,9},{9,8},{10,11... | collective-permute-start | bytes 1572872 | tf_op jit(solution)/shard_map/ppermute | solution.py:192
  26.4 12.6 %collective-permute-start.12 = (bf16[256,1024]{1,0:T(8,128)(2,1)S(1)}, bf16[256,1024]{1,0:T(8,128)(2,1)S(1)}, u32[]{:S(2)}, u32[]{:S(2)}) collective-permute-start(bf16[256,1024]{1,0:T(8,128)(2,1)S(1)} %collective-permute-done.1.refs_6_), channel_id=1, source_target_pairs={{0,1},{1,0},{2,3},{3,2},{4,5},{5,4},{6,7},{7,6},{8,9},{9,8},{10,11... | collective-permute-start | bytes 1572872 | tf_op jit(solution)/shard_map/ppermute | solution.py:192
  35.5 4.9 %collective-permute-start.13 = (bf16[256,1024]{1,0:T(8,128)(2,1)S(1)}, bf16[256,1024]{1,0:T(8,128)(2,1)S(1)}, u32[]{:S(2)}, u32[]{:S(2)}) collective-permute-start(bf16[256,1024]{1,0:T(8,128)(2,1)S(1)} %collective-permute-done.3.refs_7_.refs_5_), channel_id=1, source_target_pairs={{0,1},{1,0},{2,3},{3,2},{4,5},{5,4},{6,7},{7,6},{8,9},{9,8},{10,11... | collective-permute-start | bytes 1572872 | tf_op jit(solution)/shard_map/ppermute | solution.py:192
  36.7 5.0 %collective-permute-start.14 = (bf16[256,1024]{1,0:T(8,128)(2,1)S(1)}, bf16[256,1024]{1,0:T(8,128)(2,1)S(1)}, u32[]{:S(2)}, u32[]{:S(2)}) collective-permute-start(bf16[256,1024]{1,0:T(8,128)(2,1)S(1)} %collective-permute-done.5.refs_8_), channel_id=1, source_target_pairs={{0,1},{1,0},{2,3},{3,2},{4,5},{5,4},{6,7},{7,6},{8,9},{9,8},{10,11... | collective-permute-start | bytes 1572872 | tf_op jit(solution)/shard_map/ppermute | solution.py:192
  38.3 4.6 %collective-permute-start.15 = (bf16[256,1024]{1,0:T(8,128)(2,1)S(1)}, bf16[256,1024]{1,0:T(8,128)(2,1)S(1)}, u32[]{:S(2)}, u32[]{:S(2)}) collective-permute-start(bf16[256,1024]{1,0:T(8,128)(2,1)S(1)} %collective-permute-done.6.refs_9_.refs_6_), channel_id=1, source_target_pairs={{0,1},{1,0},{2,3},{3,2},{4,5},{5,4},{6,7},{7,6},{8,9},{9,8},{10,11... | collective-permute-start | bytes 1572872 | tf_op jit(solution)/shard_map/ppermute | solution.py:192
  38.3 4.5 %collective-permute-start.16 = (bf16[256,1024]{1,0:T(8,128)(2,1)S(1)}, bf16[256,1024]{1,0:T(8,128)(2,1)S(1)}, u32[]{:S(2)}, u32[]{:S(2)}) collective-permute-start(bf16[256,1024]{1,0:T(8,128)(2,1)S(1)} %collective-permute-done.7.refs_10_), channel_id=1, source_target_pairs={{0,1},{1,0},{2,3},{3,2},{4,5},{5,4},{6,7},{7,6},{8,9},{9,8},{10,11... | collective-permute-start | bytes 1572872 | tf_op jit(solution)/shard_map/ppermute | solution.py:192
  38.9 23.4 %collective-permute-start.10 = (bf16[256,1024]{1,0:T(8,128)(2,1)S(1)}, bf16[256,1024]{1,0:T(8,128)(2,1)S(1)}, u32[]{:S(2)}, u32[]{:S(2)}) collective-permute-start(bf16[256,1024]{1,0:T(8,128)(2,1)S(1)} %get-tuple-element.45), channel_id=1, source_target_pairs={{0,8},{1,9},{2,10},{3,11},{4,12},{5,13},{6,14},{7,15},{8,16},{9,17... | collective-permute-start | bytes 1572872 | tf_op jit(solution)/shard_map/ppermute | solution.py:192
  40.4 21.9 %collective-permute-start.8 = (bf16[256,1024]{1,0:T(8,128)(2,1)S(1)}, bf16[256,1024]{1,0:T(8,128)(2,1)S(1)}, u32[]{:S(2)}, u32[]{:S(2)}) collective-permute-start(bf16[256,1024]{1,0:T(8,128)(2,1)S(1)} %collective-permute-done.6.refs_9_.refs_6_), channel_id=1, source_target_pairs={{0,2},{1,3},{2,0},{3,1},{4,6},{5,7},{6,4},{7,5},{8,10},{9,11},{10,... | collective-permute-start | bytes 1572872 | tf_op jit(solution)/shard_map/ppermute | solution.py:192
  41.7 20.6 %collective-permute-start.9 = (bf16[256,1024]{1,0:T(8,128)(2,1)S(1)}, bf16[256,1024]{1,0:T(8,128)(2,1)S(1)}, u32[]{:S(2)}, u32[]{:S(2)}) collective-permute-start(bf16[256,1024]{1,0:T(8,128)(2,1)S(1)} %broadcast_select_fusion.2), channel_id=1, source_target_pairs={{0,4},{1,5},{2,6},{3,7},{4,0},{5,1},{6,2},{7,3},{8,12},{9,13},{10,... | collective-permute-start | bytes 1572872 | tf_op jit(solution)/shard_map/ppermute | solution.py:192
  62.3 2.6 %collective-permute-start.17 = (bf16[256,1024]{1,0:T(8,128)(2,1)S(1)}, bf16[256,1024]{1,0:T(8,128)(2,1)S(1)}, u32[]{:S(2)}, u32[]{:S(2)}) collective-permute-start(bf16[256,1024]{1,0:T(8,128)(2,1)S(1)} %collective-permute-done.8.refs_7_), channel_id=1, source_target_pairs={{0,1},{1,0},{2,3},{3,2},{4,5},{5,4},{6,7},{7,6},{8,9},{9,8},{10,11... | collective-permute-start | bytes 1572872 | tf_op jit(solution)/shard_map/ppermute | solution.py:192
  63.4 2.3 %collective-permute-start.18 = (bf16[256,1024]{1,0:T(8,128)(2,1)S(1)}, bf16[256,1024]{1,0:T(8,128)(2,1)S(1)}, u32[]{:S(2)}, u32[]{:S(2)}) collective-permute-start(bf16[256,1024]{1,0:T(8,128)(2,1)S(1)} %collective-permute-done.9.refs_8_), channel_id=1, source_target_pairs={{0,1},{1,0},{2,3},{3,2},{4,5},{5,4},{6,7},{7,6},{8,9},{9,8},{10,11... | collective-permute-start | bytes 1572872 | tf_op jit(solution)/shard_map/ppermute | solution.py:192
  63.4 3.0 %collective-permute-start.19 = (bf16[256,1024]{1,0:T(8,128)(2,1)S(1)}, bf16[256,1024]{1,0:T(8,128)(2,1)S(1)}, u32[]{:S(2)}, u32[]{:S(2)}) collective-permute-start(bf16[256,1024]{1,0:T(8,128)(2,1)S(1)} %collective-permute-done.10.refs_9_), channel_id=1, source_target_pairs={{0,1},{1,0},{2,3},{3,2},{4,5},{5,4},{6,7},{7,6},{8,9},{9,8},{10,11... | collective-permute-start | bytes 1572872 | tf_op jit(solution)/shard_map/ppermute | solution.py:192
where the time goes:
time: 86 us; the launch traced here: 85.6 us
  Pallas kernels  48 us (56%)
  starting transfers between devices  16.8 us (20%)
  waiting for transfers between devices  11.7 us (14%)
  local copies, waits for them, and re-layouts  5.9 us (7%)
  other arithmetic  1.79 us (2%)
  between operations  1.34 us (2%)
    pallas_call x3, Pallas kernels, call(): pl.pallas_call(functools.partial(kernel, group), grid_spec=pltpu.Prefetch...  48 us
    ppermute x20, starting transfers between devices, send(): return lax.ppermute(array, AXES, along[way])  16.8 us
    ppermute x20, waiting for transfers between devices, send(): return lax.ppermute(array, AXES, along[way])  11.7 us
    unnamed x8, local copies, waits for them, and re-layouts  3.55 us
  transfers between devices with their start and end apart: 20, of which 4 were waited for; matrix products, arithmetic and copies ran while one was open for 5% of the time, Pallas kernels for 34%

commit v1 on v0

v1 whole, which is shorter than its diff:
```python
import functools
import math

import jax
import jax.numpy as jnp
from jax import lax
from jax.experimental import pallas as pl
from jax.experimental.pallas import tpu as pltpu
from jax.sharding import PartitionSpec as P

HEAD_DIM = 128
REACH = 8
AXES = ("section", "attn")
NEG = -1e30
SCALE = HEAD_DIM ** -0.5 * math.log2(math.e)
HEADS_STEP = 4
VMEM_BYTES = 16 * 2**20
HIGH = 2.0 ** 60
barrier = lax.optimization_barrier


def scores(q, k):
    return lax.dot_general(q, k, (((1,), (1,)), ((), ())), preferred_element_type=jnp.float32)


def heads_of(ref, step, count):
    at = pl.multiple_of(step * (count * HEAD_DIM), HEAD_DIM)
    return [ref[:, pl.ds(at + i * HEAD_DIM, HEAD_DIM)] for i in range(count)]


def put_head(ref, step, count, i, value):
    at = pl.multiple_of(step * (count * HEAD_DIM), HEAD_DIM)
    ref[:, pl.ds(at + i * HEAD_DIM, HEAD_DIM)] = value


def with_ones(v, ok):
    return jnp.concatenate([v * ok, ok], axis=1)


def own_kernel(group, info, q_ref, start_ref, k_ref, v_ref, acc_ref, top_ref, total_ref):
    rows = q_ref.shape[0]
    count = HEADS_STEP * group

    def step(j, _):
        start = start_ref[...]
        at = lax.broadcasted_iota(jnp.int32, (rows, rows), 1)
        row = lax.broadcasted_iota(jnp.int32, (rows, rows), 0)
        allowed = (at <= row) & (at + info[0] >= start)
        sees_earlier = jnp.broadcast_to(start, (rows, HEAD_DIM)) <= info[1]
        qs = heads_of(q_ref, j, count)
        ks, vs = heads_of(k_ref, j, HEADS_STEP), heads_of(v_ref, j, HEADS_STEP)
        for i in range(count):
            s = jnp.where(allowed, scores(qs[i], ks[i // group]), NEG)
            top = jnp.max(s, axis=1, keepdims=True)
            w = jnp.exp2((s - top) * SCALE).astype(jnp.bfloat16)
            v = vs[i // group]
            both = jnp.dot(w, with_ones(v, jnp.ones_like(v)), preferred_element_type=jnp.float32)
            put_head(acc_ref, j, count, i, both[:, :HEAD_DIM])
            total_ref[j * count + i] = both[:, HEAD_DIM:]
            top_ref[j * count + i] = jnp.where(sees_earlier, jnp.broadcast_to(top, (rows, HEAD_DIM)), -NEG)
        return 0

    lax.fori_loop(0, k_ref.shape[1] // HEAD_DIM // HEADS_STEP, step, 0)


def far_kernel(group, choose, last, info, q_ref, acc_in, top_in, total_in, *refs):
    rows = q_ref.shape[0]
    if last:
        refs, (hbm, acc_out, sems) = refs[:-3], refs[-3:]
    else:
        refs, (acc_out, top_out, total_out) = refs[:-3], refs[-3:]
    count = HEADS_STEP * group
    steps = refs[0].shape[1] // HEAD_DIM // HEADS_STEP
    needed = info[1] > 0

    def put(j, i, total, out, top=None):
        if last:
            out = (out / total).astype(jnp.bfloat16)
        else:
            if top is not None:
                top_out[j * count + i] = top
            total_out[j * count + i] = total
        put_head(acc_out, j, count, i, out)

    def attend(j, exact):
        qs, befores = heads_of(q_ref, j, count), heads_of(acc_in, j, count)
        tiles = [heads_of(r, j, HEADS_STEP) for r in refs]
        at = lax.broadcasted_iota(jnp.int32, (rows, HEAD_DIM), 0)
        high = None
        for h in range(HEADS_STEP):
            ks, vs = choose(info[0], [t[h] for t in tiles])
            places = [info[3 + n] for n in range(len(ks))]
            k = jnp.concatenate(ks, axis=0)
            ok = [jnp.where(at + place >= info[2], 1.0, 0.0).astype(jnp.bfloat16) for place in places]
            v = jnp.concatenate([with_ones(v, o) for v, o in zip(vs, ok)], axis=0)
            for i in range(h * group, (h + 1) * group):
                s = scores(qs[i], k)
                top, total, before = top_in[j * count + i], total_in[j * count + i], befores[i]
                if exact:
                    key = lax.broadcasted_iota(jnp.int32, (rows, rows), 1)
                    allowed = jnp.concatenate([key + place >= info[2] for place in places], axis=1)
                    s = jnp.where(allowed, s, NEG)
                    new = jnp.maximum(top, jnp.max(s, axis=1, keepdims=True))
                    back = jnp.exp2((top - new) * SCALE)
                    top, total, before = new, total * back, before * back
                w = []
                for n in range(k.shape[0] // HEAD_DIM):
                    part = jnp.exp2((s[:, n * HEAD_DIM:(n + 1) * HEAD_DIM] - top) * SCALE).astype(jnp.bfloat16)
                    w.append(part)
                    if not exact:
                        high = part if high is None else jnp.maximum(high, part)
                both = jnp.dot(jnp.concatenate(w, axis=1), v, preferred_element_type=jnp.float32)
                put(j, i, total + both[:, HEAD_DIM:], both[:, :HEAD_DIM] + before, top if exact else None)
        return high

    def step(j, _):
        @pl.when(needed)
        def _():
            high = attend(j, False)

            @pl.when(jnp.max(high.astype(jnp.float32)) > HIGH)
            def _():
                attend(j, True)

        @pl.when(jnp.logical_not(needed))
        def _():
            for i, before in enumerate(heads_of(acc_in, j, count)):
                put(j, i, total_in[j * count + i], before)

        if last:
            part(j).start()
        return 0

    def part(j):
        width = count * HEAD_DIM
        columns = pl.ds(pl.multiple_of(j * width, width), width)
        return pltpu.make_async_copy(acc_out.at[:, columns], hbm.at[:, columns], sems.at[j])

    lax.fori_loop(0, steps, step, 0)
    if last:
        for j in range(steps):
            part(j).wait()


def pick(plane, at0, at1, at2, at3):
    return jnp.where(plane == 0, at0, jnp.where(plane == 1, at1, jnp.where(plane == 2, at2, at3)))


def choose_first(core, tiles):
    mate_k, mate_v, odd_k, odd_v = tiles
    return (jnp.where(core == 1, mate_k, odd_k),), (jnp.where(core == 1, mate_v, odd_v),)


def choose_middle(plane, tiles):
    def half(x1, y1, x2, y2, z2):
        pk, pv = pick(plane, x2, x2, y2, x2), pick(plane, z2, x1, y1, x1)
        qk, qv = pick(plane, y2, y2, x2, y2), pick(plane, z2, z2, z2, y1)
        return pk, pv, qk, qv
    a, b = half(*tiles[:5]), half(*tiles[5:])
    return (a[0], b[0], a[2], b[2]), (a[1], b[1], a[3], b[3])


def choose_last(plane, tiles):
    def half(z1, y2, x3, y3, z3):
        pk, pv = pick(plane, y2, x3, x3, x3), pick(plane, z3, y3, y3, y3)
        qk, qv = pick(plane, x3, z1, z1, z1), pick(plane, y3, z3, z3, z3)
        return pk, pv, qk, qv
    a, b = half(*tiles[:5]), half(*tiles[5:])
    return (a[0], b[0], a[2], b[2]), (a[1], b[1], a[3], b[3])


def call(kernel, info, q, start, carry, pieces, last, keys):
    rows, width = q.shape
    steps = pieces[0].shape[1] // HEAD_DIM // HEADS_STEP
    group = width // pieces[0].shape[1]
    vmem = pl.BlockSpec(memory_space=pltpu.VMEM)
    arrays = [q, *start, *carry, *pieces]
    if last:
        out_shape = [jax.ShapeDtypeStruct(q.shape, jnp.bfloat16)]
        scratch = [pltpu.VMEM(q.shape, jnp.bfloat16), pltpu.SemaphoreType.DMA((steps,))]
    else:
        out_shape = [jax.ShapeDtypeStruct(q.shape, jnp.float32)]
        out_shape += [jax.ShapeDtypeStruct((width // HEAD_DIM, rows, HEAD_DIM), jnp.float32)] * 2
        scratch = []
    return pl.pallas_call(
        functools.partial(kernel, group),
        in_specs=[pl.BlockSpec(memory_space=pltpu.SMEM)] + [vmem] * len(arrays),
        out_specs=[pl.BlockSpec(memory_space=pl.ANY) if last else vmem] * len(out_shape),
        out_shape=out_shape,
        scratch_shapes=scratch,
        input_output_aliases={3: 1} if carry and not last else {},
        cost_estimate=pl.CostEstimate(
            flops=8 * rows * keys * width, bytes_accessed=4 * rows * width, transcendentals=0
        ),
        compiler_params=pltpu.CompilerParams(vmem_limit_bytes=VMEM_BYTES),
    )(info, *arrays)


def shards(queries, keys, values, doc_ids):
    rows = queries.shape[0]
    chips, cores = lax.axis_size("section"), lax.axis_size("attn")
    chip, core = lax.axis_index("section"), lax.axis_index("attn")
    owner = chip * cores + core
    plane, odd_x, odd_y = chip % 4, chip % 2, (chip // 2) % 2

    def routes(target):
        return [(c * cores + k, target(c) * cores + k) for c in range(chips) for k in range(cores)]

    along = {"x": routes(lambda c: c ^ 1), "y": routes(lambda c: c ^ 2), "z": routes(lambda c: (c + 4) % chips)}
    along["mate"] = [(c * cores + k, c * cores + 1 - k) for c in range(chips) for k in range(cores)]

    def send(array, way):
        return lax.ppermute(array, AXES, along[way])

    def swap(*arrays):
        return tuple(send(a, "mate") for a in arrays)

    first = owner * rows
    span = min(REACH * rows, doc_ids.shape[0])
    low = jnp.maximum(first - (REACH - 1) * rows, 0)
    window = lax.dynamic_slice_in_dim(doc_ids, low, span)
    query_doc = lax.dynamic_slice_in_dim(doc_ids, first, rows)
    start = low + jnp.sum((window[None, :] < query_doc[:, None]).astype(jnp.int32), axis=1, keepdims=True)
    none = jnp.int32(-(2**30))

    def place(device, ok=True):
        return jnp.where((device >= 0) & (device < owner) & ok, device * rows, none)

    def info_of(choice, places):
        newest = functools.reduce(jnp.maximum, places)
        needed = (newest + rows > start[0, 0]).astype(jnp.int32)
        return jnp.stack([choice, needed, start[0, 0]] + places)

    def halves(back):
        base = (chip - back) * cores
        return [place(base + core), place(base + 1 - core)]

    own_info = jnp.stack([first, start[0, 0]])
    first_info = info_of(core, [jnp.where(core == 1, place(owner - 1), place(owner - 7, plane == 0))])
    q_places = [jnp.where(plane == 0, none, p) for p in halves(pick(plane, 0, 2, 3, 2))]
    middle_info = info_of(plane, halves(pick(plane, 3, 1, 2, 1)) + q_places)
    last_info = info_of(plane, halves(pick(plane, 2, 3, 1, 3)) + halves(pick(plane, 1, 4, 4, 4)))

    w = jnp.where
    mate_k, mate_v = swap(keys, values)
    x1, y1 = send(values, "x"), send(values, "y")
    z1 = send(w((plane == 0) & (core == 0), mate_v, keys), "z")
    carry = call(own_kernel, own_info, queries, (start,), (), [keys, values], False, rows)
    x1, y1, z1, mate_k, mate_v, first_info, middle_info, last_info, *carry = barrier(
        (x1, y1, z1, mate_k, mate_v, first_info, middle_info, last_info, *carry)
    )
    x2 = send(w(odd_x == 0, keys, z1), "x")
    y2 = send(w(odd_y == 0, keys, z1), "y")
    z2 = send(w(plane == 1, y1, x1), "z")
    x1s, y1s, z1s = swap(x1, y1, z1)
    carry = call(
        lambda group, *refs: far_kernel(group, choose_first, False, *refs),
        first_info, queries, (), carry, [mate_k, mate_v, z1s, z1], False, rows,
    )
    x2, y2, z2, *carry = barrier((x2, y2, z2, *carry))
    x3 = send(y2, "x")
    y3 = send(w(odd_y == 0, x1, z2), "y")
    z3 = send(w(plane == 0, y1, values), "z")
    x2s, y2s, z2s = swap(x2, y2, z2)
    carry = call(
        lambda group, *refs: far_kernel(group, choose_middle, False, *refs),
        middle_info, queries, (), carry,
        [x1, y1, x2, y2, z2, x1s, y1s, x2s, y2s, z2s], False, 4 * rows,
    )
    x3, y3, z3, *carry = barrier((x3, y3, z3, *carry))
    x3s, y3s, z3s = swap(x3, y3, z3)
    (out,) = call(
        lambda group, *refs: far_kernel(group, choose_last, True, *refs),
        last_info, queries, (), carry,
        [z1, y2, x3, y3, z3, z1s, y2s, x3s, y3s, z3s], True, 4 * rows,
    )
    return out


def solution(mesh):
    split = P(AXES, None)
    return jax.shard_map(
        shards, mesh=mesh, in_specs=(split, split, split, P()), out_specs=split, check_vma=False
    )
```

time: 86 us -> 68.4 us (0.80)
  the two profiles are of different devices: /device:TPU:13 before, /device:TPU:4 now
where the time goes in v1:
time: 68.4 us; the launch traced here: 68 us
  waiting for transfers between devices  30.1 us (44%)
  Pallas kernels  15.9 us (23%)
  starting transfers between devices  9.84 us (14%)
  local copies, waits for them, and re-layouts  6.99 us (10%)
  other arithmetic  3.01 us (4%)
  between operations  2.19 us (3%)
    ppermute x20, waiting for transfers between devices, send(): return lax.ppermute(array, AXES, along[way])  30.1 us
    pallas_call x4, Pallas kernels, call(): pl.pallas_call(functools.partial(kernel, group), in_specs=[pl.BlockSpec(m...  15.9 us
    ppermute x20, starting transfers between devices, send(): return lax.ppermute(array, AXES, along[way])  9.84 us
    unnamed x6, local copies, waits for them, and re-layouts  3.49 us
  transfers between devices with their start and end apart: 20, of which 7 were waited for; matrix products, arithmetic and copies ran while one was open for 10% of the time, Pallas kernels for 9%

profile of v1, /device:TPU:4, one launch (start us, length us, event | category | flops | bytes accessed | tf_op | source)
XLA Modules:
  0.0 68.0 jit_solution(13063123777509495693)
XLA Ops:
  0.0 0.0 collective-permute-start.2
  0.0 1.5 %collective-permute-start = (bf16[256,1024]{1,0:T(8,128)(2,1)}, bf16[256,1024]{1,0:T(8,128)(2,1)S(1)}, u32[]{:S(2)}, u32[]{:S(2)}) collective-permute-start(bf16[256,1024]{1,0:T(8,128)(2,1)} %v_ref.1), channel_id=1, source_target_pairs={{0,2},{1,3},{2,0},{3,1},{4,6},{5,7},{6,4},{7,5},{8,10},{9,11},{10,... | collective-permute-start | bytes 1572872 | tf_op jit(solution)/shard_map/ppermute | solution.py:213
  1.5 0.5 collective-permute-start.1
  2.0 0.0 collective-permute-start.4
  2.0 0.8 %dynamic_slice.7 = s32[256]{0:T(256)S(1)} dynamic-slice(s32[8192]{0:T(1024)} %param.7, s32[]{:T(128)S(6)} %select_n.138), dynamic_slice_sizes={256} | dynamic-slice | bytes 2052 | tf_op jit(solution)/shard_map/dynamic_slice | solution.py:222
  2.8 0.8 %dynamic_slice.6 = s32[2048]{0:T(1024)S(1)} dynamic-slice(s32[8192]{0:T(1024)} %param.7, s32[]{:T(128)S(6)} %max.21), dynamic_slice_sizes={2048} | dynamic-slice | bytes 16388 | tf_op jit(solution)/shard_map/dynamic_slice | solution.py:221
  3.5 0.4 convert_reduce_fusion
  3.9 0.0 collective-permute-done.2.refs_6_
  3.9 1.1 %broadcast_select_fusion.5 = bf16[256,1024]{1,0:T(8,128)(2,1)S(1)} fusion(bf16[256,1024]{1,0:T(8,128)(2,1)S(1)} %collective-permute-done.2.refs_6_, bf16[256,1024]{1,0:T(8,128)(2,1)} %k_ref.1, pred[]{:T(512)S(6)} %and.57), kind=kLoop, calls=%fused_computation.6 | loop fusion | flops 262144 | bytes 1572865 | tf_op jit(solution)/shard_map/jit(_where)/select_n | solution.py:247
  5.0 1.6 %collective-permute-start.3 = (bf16[256,1024]{1,0:T(8,128)(2,1)S(1)}, bf16[256,1024]{1,0:T(8,128)(2,1)S(1)}, u32[]{:S(2)}, u32[]{:S(2)}) collective-permute-start(bf16[256,1024]{1,0:T(8,128)(2,1)S(1)} %broadcast_select_fusion.5), channel_id=1, source_target_pairs={{0,8},{1,9},{2,10},{3,11},{4,12},{5,13},{6,14},{7,15},{8,16},{9,17... | collective-permute-start | bytes 1572872 | tf_op jit(solution)/shard_map/ppermute | solution.py:213
  6.7 0.5 slice.3
  7.2 0.1 copy.8.start_ref
  9.2 0.7 stack.86.refs_0_
  9.8 0.7 stack.79.refs_0_
  10.5 0.6 pad_add_fusion.1.info
  11.1 0.6 pad_add_fusion.refs_0_
  11.8 0.0 copy-start
  11.8 1.0 %copy-done = bf16[256,1024]{1,0:T(8,128)(2,1)S(1)} copy-done((bf16[256,1024]{1,0:T(8,128)(2,1)S(1)}, bf16[256,1024]{1,0:T(8,128)(2,1)}, u32[]{:S(2)}) %copy-start) | copy-done | bytes 524312
  12.8 0.0 copy-start.1
  12.8 1.4 %copy-done.1 = bf16[256,3072]{1,0:T(8,128)(2,1)S(1)} copy-done((bf16[256,3072]{1,0:T(8,128)(2,1)S(1)}, bf16[256,3072]{1,0:T(8,128)(2,1)}, u32[]{:S(2)}) %copy-start.1) | copy-done | bytes 1572888
  14.2 0.0 copy-start.2
  14.2 1.0 %copy-done.2 = bf16[256,1024]{1,0:T(8,128)(2,1)S(1)} copy-done((bf16[256,1024]{1,0:T(8,128)(2,1)S(1)}, bf16[256,1024]{1,0:T(8,128)(2,1)}, u32[]{:S(2)}) %copy-start.2) | copy-done | bytes 524312
  15.3 3.2 %shard_map.46 = (f32[256,3072]{1,0:T(8,128)S(1)}, f32[24,256,128]{2,1,0:T(8,128)S(1)}, f32[24,256,128]{2,1,0:T(8,128)S(1)}) custom-call(s32[2]{0:T(128)S(1)} %pad_add_fusion.1.info, bf16[256,3072]{1,0:T(8,128)(2,1)S(1)} %copy-done.1, s32[256,1]{1,0:T(8,128)S(1)} %copy.8.start_ref, bf16[256,1024]{1,0:T(8,128)(2,1)S(1)} %copy-done, bf16[256,1024]{1,0:T(8,128)(2,1)S(1)} %copy-done.2), custom_call_target="tpu_custom_call" | custom-call | flops 1610612736 | bytes 3145728 | tf_op jit(solution)/shard_map/pallas_call | solution.py:185
  18.5 0.0 collective-permute-done.refs_5_
  18.5 0.0 collective-permute-done.1.refs_6_
  18.5 0.0 collective-permute-done.4.refs_5_
  18.5 2.8 %collective-permute-done.3.refs_8_.refs_5_ = bf16[256,1024]{1,0:T(8,128)(2,1)S(1)} collective-permute-done((bf16[256,1024]{1,0:T(8,128)(2,1)S(1)}, bf16[256,1024]{1,0:T(8,128)(2,1)S(1)}, u32[]{:S(2)}, u32[]{:S(2)}) %collective-permute-start.3) | collective-permute-done | bytes 524320 | tf_op jit(solution)/shard_map/ppermute | solution.py:213
  21.3 0.0 collective-permute-start.8
  21.3 0.1 broadcast_select_fusion
  21.4 0.1 collective-permute-start.7
  21.5 0.1 broadcast_select_fusion.3
  21.5 0.6 collective-permute-start.5
  22.1 1.5 %collective-permute-start.6 = (bf16[256,1024]{1,0:T(8,128)(2,1)S(1)}, bf16[256,1024]{1,0:T(8,128)(2,1)S(1)}, u32[]{:S(2)}, u32[]{:S(2)}) collective-permute-start(bf16[256,1024]{1,0:T(8,128)(2,1)S(1)} %get-tuple-element.69), channel_id=1, source_target_pairs={{0,4},{1,5},{2,6},{3,7},{4,0},{5,1},{6,2},{7,3},{8,12},{9,13},{10,... | collective-permute-start | bytes 1572872 | tf_op jit(solution)/shard_map/ppermute | solution.py:213
  23.7 0.0 collective-permute-start.12
  23.7 0.0 collective-permute-done.8.refs_7_.refs_10_
  23.7 0.5 collective-permute-start.13
  24.2 1.4 %shard_map.47 = (f32[256,3072]{1,0:T(8,128)S(1)}, f32[24,256,128]{2,1,0:T(8,128)S(1)}, f32[24,256,128]{2,1,0:T(8,128)S(1)}) custom-call(s32[4]{0:T(128)S(1)} %pad_add_fusion.refs_0_, bf16[256,3072]{1,0:T(8,128)(2,1)S(1)} %copy-done.1, f32[256,3072]{1,0:T(8,128)S(1)} %get-tuple-element.45.refs_2_, ...), custom_call_target="tpu_custom_call", output_to_operand_aliasing={{1}: (3, {})} | custom-call | flops 1610612736 | bytes 3145728 | tf_op jit(solution)/shard_map/pallas_call | solution.py:185
  25.6 12.0 %collective-permute-done.7.refs_9_ = bf16[256,1024]{1,0:T(8,128)(2,1)S(1)} collective-permute-done((bf16[256,1024]{1,0:T(8,128)(2,1)S(1)}, bf16[256,1024]{1,0:T(8,128)(2,1)S(1)}, u32[]{:S(2)}, u32[]{:S(2)}) %collective-permute-start.7) | collective-permute-done | bytes 524320 | tf_op jit(solution)/shard_map/ppermute | solution.py:213
  37.6 0.0 collective-permute-done.5.refs_7_
  37.6 0.0 collective-permute-done.6.refs_8_.refs_6_
  37.6 0.0 collective-permute-start.14
  37.6 0.5 collective-permute-start.15
  38.1 0.1 collective-permute-start.16
  38.2 0.1 broadcast_select_fusion.2
  38.2 0.0 collective-permute-done.12.refs_10_
  38.2 0.2 collective-permute-start.11
  38.5 0.0 collective-permute-done.13.refs_11_
  38.5 1.0 %collective-permute-start.9 = (bf16[256,1024]{1,0:T(8,128)(2,1)S(1)}, bf16[256,1024]{1,0:T(8,128)(2,1)S(1)}, u32[]{:S(2)}, u32[]{:S(2)}) collective-permute-start(bf16[256,1024]{1,0:T(8,128)(2,1)S(1)} %collective-permute-done.6.refs_8_.refs_6_), channel_id=1, source_target_pairs={{0,2},{1,3},{2,0},{3,1},{4,6},{5,7},{6,4},{7,5},{8,10},{9,11},{10,... | collective-permute-start | bytes 1572872 | tf_op jit(solution)/shard_map/ppermute | solution.py:213
  39.5 0.0 collective-permute-done.14.refs_12_
  39.5 1.1 %collective-permute-start.10 = (bf16[256,1024]{1,0:T(8,128)(2,1)S(1)}, bf16[256,1024]{1,0:T(8,128)(2,1)S(1)}, u32[]{:S(2)}, u32[]{:S(2)}) collective-permute-start(bf16[256,1024]{1,0:T(8,128)(2,1)S(1)} %broadcast_select_fusion.2), channel_id=1, source_target_pairs={{0,4},{1,5},{2,6},{3,7},{4,0},{5,1},{6,2},{7,3},{8,12},{9,13},{10,... | collective-permute-start | bytes 1572872 | tf_op jit(solution)/shard_map/ppermute | solution.py:213
  40.6 0.0 collective-permute-done.15.refs_13_.refs_11_
  40.6 0.4 collective-permute-done.16.refs_14_
  41.0 1.4 %shard_map.48 = (f32[256,3072]{1,0:T(8,128)S(1)}, f32[24,256,128]{2,1,0:T(8,128)S(1)}, f32[24,256,128]{2,1,0:T(8,128)S(1)}) custom-call(s32[7]{0:T(128)S(1)} %stack.79.refs_0_, bf16[256,3072]{1,0:T(8,128)(2,1)S(1)} %copy-done.1, f32[256,3072]{1,0:T(8,128)S(1)} %get-tuple-element.56.refs_2_, ...), custom_call_target="tpu_custom_call", output_to_operand_aliasing={{1}: (3, {})} | custom-call | flops 6442450944 | bytes 3145728 | tf_op jit(solution)/shard_map/pallas_call | solution.py:185
  42.4 12.1 %collective-permute-done.11.refs_9_ = bf16[256,1024]{1,0:T(8,128)(2,1)S(1)} collective-permute-done((bf16[256,1024]{1,0:T(8,128)(2,1)S(1)}, bf16[256,1024]{1,0:T(8,128)(2,1)S(1)}, u32[]{:S(2)}, u32[]{:S(2)}) %collective-permute-start.11) | collective-permute-done | bytes 524320 | tf_op jit(solution)/shard_map/ppermute | solution.py:213
  54.5 0.0 collective-permute-done.10.refs_8_
  54.5 0.0 collective-permute-done.9.refs_7_
  54.6 0.0 collective-permute-start.17
  54.6 0.5 collective-permute-start.18
  55.1 0.1 collective-permute-start.19
  55.1 1.3 %collective-permute-done.17.refs_12_ = bf16[256,1024]{1,0:T(8,128)(2,1)S(1)} collective-permute-done((bf16[256,1024]{1,0:T(8,128)(2,1)S(1)}, bf16[256,1024]{1,0:T(8,128)(2,1)S(1)}, u32[]{:S(2)}, u32[]{:S(2)}) %collective-permute-start.17) | collective-permute-done | bytes 524320 | tf_op jit(solution)/shard_map/ppermute | solution.py:213
  56.5 0.7 %collective-permute-done.18.refs_13_ = bf16[256,1024]{1,0:T(8,128)(2,1)S(1)} collective-permute-done((bf16[256,1024]{1,0:T(8,128)(2,1)S(1)}, bf16[256,1024]{1,0:T(8,128)(2,1)S(1)}, u32[]{:S(2)}, u32[]{:S(2)}) %collective-permute-start.18) | collective-permute-done | bytes 524320 | tf_op jit(solution)/shard_map/ppermute | solution.py:213
  57.2 0.7 %collective-permute-done.19.refs_14_ = bf16[256,1024]{1,0:T(8,128)(2,1)S(1)} collective-permute-done((bf16[256,1024]{1,0:T(8,128)(2,1)S(1)}, bf16[256,1024]{1,0:T(8,128)(2,1)S(1)}, u32[]{:S(2)}, u32[]{:S(2)}) %collective-permute-start.19) | collective-permute-done | bytes 524320 | tf_op jit(solution)/shard_map/ppermute | solution.py:213
  58.0 9.9 %shard_map.49 = bf16[256,3072]{1,0:T(8,128)(2,1)} custom-call(s32[7]{0:T(128)S(1)} %stack.86.refs_0_, bf16[256,3072]{1,0:T(8,128)(2,1)S(1)} %copy-done.1, f32[256,3072]{1,0:T(8,128)S(1)} %get-tuple-element.63.refs_2_, f32[24,256,128]{2,1,0:T(8,128)S(1)} %get-tuple-element.64.refs_3_, f32[24,256,128]{2,1,0:T(8,128)S(1)} %get-tuple-element.65.refs_4_, ...), custom_call_target="tpu_custom_call" | custom-call | flops 6442450944 | bytes 3145728 | tf_op jit(solution)/shard_map/pallas_call | solution.py:185
  (1 shorter events, 0.0 us)
Async XLA Ops:
  0.0 3.9 %collective-permute-start.2 = (bf16[256,1024]{1,0:T(8,128)(2,1)}, bf16[256,1024]{1,0:T(8,128)(2,1)S(1)}, u32[]{:S(2)}, u32[]{:S(2)}) collective-permute-start(bf16[256,1024]{1,0:T(8,128)(2,1)} %v_ref.1), channel_id=1, source_target_pairs={{0,1},{1,0},{2,3},{3,2},{4,5},{5,4},{6,7},{7,6},{8,9},{9,8},{10,11... | collective-permute-start | bytes 1572872 | tf_op jit(solution)/shard_map/ppermute | solution.py:213
  0.0 18.5 %collective-permute-start = (bf16[256,1024]{1,0:T(8,128)(2,1)}, bf16[256,1024]{1,0:T(8,128)(2,1)S(1)}, u32[]{:S(2)}, u32[]{:S(2)}) collective-permute-start(bf16[256,1024]{1,0:T(8,128)(2,1)} %v_ref.1), channel_id=1, source_target_pairs={{0,2},{1,3},{2,0},{3,1},{4,6},{5,7},{6,4},{7,5},{8,10},{9,11},{10,... | collective-permute-start | bytes 1572872 | tf_op jit(solution)/shard_map/ppermute | solution.py:213
  1.5 17.0 %collective-permute-start.1 = (bf16[256,1024]{1,0:T(8,128)(2,1)}, bf16[256,1024]{1,0:T(8,128)(2,1)S(1)}, u32[]{:S(2)}, u32[]{:S(2)}) collective-permute-start(bf16[256,1024]{1,0:T(8,128)(2,1)} %v_ref.1), channel_id=1, source_target_pairs={{0,4},{1,5},{2,6},{3,7},{4,0},{5,1},{6,2},{7,3},{8,12},{9,13},{10,... | collective-permute-start | bytes 1572872 | tf_op jit(solution)/shard_map/ppermute | solution.py:213
  2.0 16.5 %collective-permute-start.4 = (bf16[256,1024]{1,0:T(8,128)(2,1)}, bf16[256,1024]{1,0:T(8,128)(2,1)S(1)}, u32[]{:S(2)}, u32[]{:S(2)}) collective-permute-start(bf16[256,1024]{1,0:T(8,128)(2,1)} %k_ref.1), channel_id=1, source_target_pairs={{0,1},{1,0},{2,3},{3,2},{4,5},{5,4},{6,7},{7,6},{8,9},{9,8},{10,11... | collective-permute-start | bytes 1572872 | tf_op jit(solution)/shard_map/ppermute | solution.py:213
  5.0 16.2 %collective-permute-start.3 = (bf16[256,1024]{1,0:T(8,128)(2,1)S(1)}, bf16[256,1024]{1,0:T(8,128)(2,1)S(1)}, u32[]{:S(2)}, u32[]{:S(2)}) collective-permute-start(bf16[256,1024]{1,0:T(8,128)(2,1)S(1)} %broadcast_select_fusion.5), channel_id=1, source_target_pairs={{0,8},{1,9},{2,10},{3,11},{4,12},{5,13},{6,14},{7,15},{8,16},{9,17... | collective-permute-start | bytes 1572872 | tf_op jit(solution)/shard_map/ppermute | solution.py:213
  11.8 1.0 %copy-start = (bf16[256,1024]{1,0:T(8,128)(2,1)S(1)}, bf16[256,1024]{1,0:T(8,128)(2,1)}, u32[]{:S(2)}) copy-start(bf16[256,1024]{1,0:T(8,128)(2,1)} %k_ref.1) | copy-start | bytes 1572868
  12.8 1.4 %copy-start.1 = (bf16[256,3072]{1,0:T(8,128)(2,1)S(1)}, bf16[256,3072]{1,0:T(8,128)(2,1)}, u32[]{:S(2)}) copy-start(bf16[256,3072]{1,0:T(8,128)(2,1)} %refs_1_.5) | copy-start | bytes 4718596
  14.2 1.0 %copy-start.2 = (bf16[256,1024]{1,0:T(8,128)(2,1)S(1)}, bf16[256,1024]{1,0:T(8,128)(2,1)}, u32[]{:S(2)}) copy-start(bf16[256,1024]{1,0:T(8,128)(2,1)} %v_ref.1) | copy-start | bytes 1572868
  21.3 2.4 %collective-permute-start.8 = (bf16[256,1024]{1,0:T(8,128)(2,1)S(1)}, bf16[256,1024]{1,0:T(8,128)(2,1)S(1)}, u32[]{:S(2)}, u32[]{:S(2)}) collective-permute-start(bf16[256,1024]{1,0:T(8,128)(2,1)S(1)} %collective-permute-done.3.refs_8_.refs_5_), channel_id=1, source_target_pairs={{0,1},{1,0},{2,3},{3,2},{4,5},{5,4},{6,7},{7,6},{8,9},{9,8},{10,11... | collective-permute-start | bytes 1572872 | tf_op jit(solution)/shard_map/ppermute | solution.py:213
  21.4 16.2 %collective-permute-start.7 = (bf16[256,1024]{1,0:T(8,128)(2,1)S(1)}, bf16[256,1024]{1,0:T(8,128)(2,1)S(1)}, u32[]{:S(2)}, u32[]{:S(2)}) collective-permute-start(bf16[256,1024]{1,0:T(8,128)(2,1)S(1)} %get-tuple-element.72), channel_id=1, source_target_pairs={{0,8},{1,9},{2,10},{3,11},{4,12},{5,13},{6,14},{7,15},{8,16},{9,17... | collective-permute-start | bytes 1572872 | tf_op jit(solution)/shard_map/ppermute | solution.py:213
  21.5 16.0 %collective-permute-start.5 = (bf16[256,1024]{1,0:T(8,128)(2,1)S(1)}, bf16[256,1024]{1,0:T(8,128)(2,1)S(1)}, u32[]{:S(2)}, u32[]{:S(2)}) collective-permute-start(bf16[256,1024]{1,0:T(8,128)(2,1)S(1)} %get-tuple-element.70), channel_id=1, source_target_pairs={{0,2},{1,3},{2,0},{3,1},{4,6},{5,7},{6,4},{7,5},{8,10},{9,11},{10,... | collective-permute-start | bytes 1572872 | tf_op jit(solution)/shard_map/ppermute | solution.py:213
  22.1 15.5 %collective-permute-start.6 = (bf16[256,1024]{1,0:T(8,128)(2,1)S(1)}, bf16[256,1024]{1,0:T(8,128)(2,1)S(1)}, u32[]{:S(2)}, u32[]{:S(2)}) collective-permute-start(bf16[256,1024]{1,0:T(8,128)(2,1)S(1)} %get-tuple-element.69), channel_id=1, source_target_pairs={{0,4},{1,5},{2,6},{3,7},{4,0},{5,1},{6,2},{7,3},{8,12},{9,13},{10,... | collective-permute-start | bytes 1572872 | tf_op jit(solution)/shard_map/ppermute | solution.py:213
  23.7 14.6 %collective-permute-start.12 = (bf16[256,1024]{1,0:T(8,128)(2,1)S(1)}, bf16[256,1024]{1,0:T(8,128)(2,1)S(1)}, u32[]{:S(2)}, u32[]{:S(2)}) collective-permute-start(bf16[256,1024]{1,0:T(8,128)(2,1)S(1)} %collective-permute-done.refs_5_), channel_id=1, source_target_pairs={{0,1},{1,0},{2,3},{3,2},{4,5},{5,4},{6,7},{7,6},{8,9},{9,8},{10,11... | collective-permute-start | bytes 1572872 | tf_op jit(solution)/shard_map/ppermute | solution.py:213
  23.7 14.8 %collective-permute-start.13 = (bf16[256,1024]{1,0:T(8,128)(2,1)S(1)}, bf16[256,1024]{1,0:T(8,128)(2,1)S(1)}, u32[]{:S(2)}, u32[]{:S(2)}) collective-permute-start(bf16[256,1024]{1,0:T(8,128)(2,1)S(1)} %collective-permute-done.1.refs_6_), channel_id=1, source_target_pairs={{0,1},{1,0},{2,3},{3,2},{4,5},{5,4},{6,7},{7,6},{8,9},{9,8},{10,11... | collective-permute-start | bytes 1572872 | tf_op jit(solution)/shard_map/ppermute | solution.py:213
  37.6 1.9 %collective-permute-start.14 = (bf16[256,1024]{1,0:T(8,128)(2,1)S(1)}, bf16[256,1024]{1,0:T(8,128)(2,1)S(1)}, u32[]{:S(2)}, u32[]{:S(2)}) collective-permute-start(bf16[256,1024]{1,0:T(8,128)(2,1)S(1)} %collective-permute-done.5.refs_7_), channel_id=1, source_target_pairs={{0,1},{1,0},{2,3},{3,2},{4,5},{5,4},{6,7},{7,6},{8,9},{9,8},{10,11... | collective-permute-start | bytes 1572872 | tf_op jit(solution)/shard_map/ppermute | solution.py:213
  37.6 3.0 %collective-permute-start.15 = (bf16[256,1024]{1,0:T(8,128)(2,1)S(1)}, bf16[256,1024]{1,0:T(8,128)(2,1)S(1)}, u32[]{:S(2)}, u32[]{:S(2)}) collective-permute-start(bf16[256,1024]{1,0:T(8,128)(2,1)S(1)} %collective-permute-done.6.refs_8_.refs_6_), channel_id=1, source_target_pairs={{0,1},{1,0},{2,3},{3,2},{4,5},{5,4},{6,7},{7,6},{8,9},{9,8},{10,11... | collective-permute-start | bytes 1572872 | tf_op jit(solution)/shard_map/ppermute | solution.py:213
  38.1 2.9 %collective-permute-start.16 = (bf16[256,1024]{1,0:T(8,128)(2,1)S(1)}, bf16[256,1024]{1,0:T(8,128)(2,1)S(1)}, u32[]{:S(2)}, u32[]{:S(2)}) collective-permute-start(bf16[256,1024]{1,0:T(8,128)(2,1)S(1)} %collective-permute-done.7.refs_9_), channel_id=1, source_target_pairs={{0,1},{1,0},{2,3},{3,2},{4,5},{5,4},{6,7},{7,6},{8,9},{9,8},{10,11... | collective-permute-start | bytes 1572872 | tf_op jit(solution)/shard_map/ppermute | solution.py:213
  38.2 16.3 %collective-permute-start.11 = (bf16[256,1024]{1,0:T(8,128)(2,1)S(1)}, bf16[256,1024]{1,0:T(8,128)(2,1)S(1)}, u32[]{:S(2)}, u32[]{:S(2)}) collective-permute-start(bf16[256,1024]{1,0:T(8,128)(2,1)S(1)} %get-tuple-element.71), channel_id=1, source_target_pairs={{0,8},{1,9},{2,10},{3,11},{4,12},{5,13},{6,14},{7,15},{8,16},{9,17... | collective-permute-start | bytes 1572872 | tf_op jit(solution)/shard_map/ppermute | solution.py:213
  38.5 16.0 %collective-permute-start.9 = (bf16[256,1024]{1,0:T(8,128)(2,1)S(1)}, bf16[256,1024]{1,0:T(8,128)(2,1)S(1)}, u32[]{:S(2)}, u32[]{:S(2)}) collective-permute-start(bf16[256,1024]{1,0:T(8,128)(2,1)S(1)} %collective-permute-done.6.refs_8_.refs_6_), channel_id=1, source_target_pairs={{0,2},{1,3},{2,0},{3,1},{4,6},{5,7},{6,4},{7,5},{8,10},{9,11},{10,... | collective-permute-start | bytes 1572872 | tf_op jit(solution)/shard_map/ppermute | solution.py:213
  39.5 15.0 %collective-permute-start.10 = (bf16[256,1024]{1,0:T(8,128)(2,1)S(1)}, bf16[256,1024]{1,0:T(8,128)(2,1)S(1)}, u32[]{:S(2)}, u32[]{:S(2)}) collective-permute-start(bf16[256,1024]{1,0:T(8,128)(2,1)S(1)} %broadcast_select_fusion.2), channel_id=1, source_target_pairs={{0,4},{1,5},{2,6},{3,7},{4,0},{5,1},{6,2},{7,3},{8,12},{9,13},{10,... | collective-permute-start | bytes 1572872 | tf_op jit(solution)/shard_map/ppermute | solution.py:213
  54.6 1.9 %collective-permute-start.17 = (bf16[256,1024]{1,0:T(8,128)(2,1)S(1)}, bf16[256,1024]{1,0:T(8,128)(2,1)S(1)}, u32[]{:S(2)}, u32[]{:S(2)}) collective-permute-start(bf16[256,1024]{1,0:T(8,128)(2,1)S(1)} %collective-permute-done.9.refs_7_), channel_id=1, source_target_pairs={{0,1},{1,0},{2,3},{3,2},{4,5},{5,4},{6,7},{7,6},{8,9},{9,8},{10,11... | collective-permute-start | bytes 1572872 | tf_op jit(solution)/shard_map/ppermute | solution.py:213
  54.6 2.7 %collective-permute-start.18 = (bf16[256,1024]{1,0:T(8,128)(2,1)S(1)}, bf16[256,1024]{1,0:T(8,128)(2,1)S(1)}, u32[]{:S(2)}, u32[]{:S(2)}) collective-permute-start(bf16[256,1024]{1,0:T(8,128)(2,1)S(1)} %collective-permute-done.10.refs_8_), channel_id=1, source_target_pairs={{0,1},{1,0},{2,3},{3,2},{4,5},{5,4},{6,7},{7,6},{8,9},{9,8},{10,11... | collective-permute-start | bytes 1572872 | tf_op jit(solution)/shard_map/ppermute | solution.py:213
  55.1 2.9 %collective-permute-start.19 = (bf16[256,1024]{1,0:T(8,128)(2,1)S(1)}, bf16[256,1024]{1,0:T(8,128)(2,1)S(1)}, u32[]{:S(2)}, u32[]{:S(2)}) collective-permute-start(bf16[256,1024]{1,0:T(8,128)(2,1)S(1)} %collective-permute-done.11.refs_9_), channel_id=1, source_target_pairs={{0,1},{1,0},{2,3},{3,2},{4,5},{5,4},{6,7},{7,6},{8,9},{9,8},{10,11... | collective-permute-start | bytes 1572872 | tf_op jit(solution)/shard_map/ppermute | solution.py:213

commit v2 on v1

v2 whole, which is shorter than its diff:
```python
import functools
import math

import jax
import jax.numpy as jnp
from jax import lax
from jax.experimental import pallas as pl
from jax.experimental.pallas import tpu as pltpu
from jax.sharding import PartitionSpec as P

HEAD_DIM = 128
REACH = 8
AXES = ("section", "attn")
NEG = -1e30
SCALE = HEAD_DIM ** -0.5 * math.log2(math.e)
HEADS_STEP = 4
VMEM_BYTES = 16 * 2**20
HIGH = 2.0 ** 60
barrier = lax.optimization_barrier


def scores(q, k):
    return lax.dot_general(q, k, (((1,), (1,)), ((), ())), preferred_element_type=jnp.float32)


def heads_of(ref, step, count):
    at = pl.multiple_of(step * (count * HEAD_DIM), HEAD_DIM)
    return [ref[:, pl.ds(at + i * HEAD_DIM, HEAD_DIM)] for i in range(count)]


def put_head(ref, step, count, i, value):
    at = pl.multiple_of(step * (count * HEAD_DIM), HEAD_DIM)
    ref[:, pl.ds(at + i * HEAD_DIM, HEAD_DIM)] = value


def with_ones(v, ok):
    return jnp.concatenate([v * ok, ok], axis=1)


def where_am_i(ids, docs_ref, rows):
    chip, core = ids[0], ids[1]
    first = (chip * ids[2] + core) * rows
    head = docs_ref[pl.ds(first // HEAD_DIM, 1), :][:, :1]
    earlier = (docs_ref[...] < head).astype(jnp.int32)
    return chip, core, first, jnp.sum(earlier), head


def own_kernel(group, ids, docs_ref, q_ref, k_ref, v_ref, acc_ref, top_ref, total_ref):
    rows = q_ref.shape[0]
    count = HEADS_STEP * group
    _, _, first, _, head = where_am_i(ids, docs_ref, rows)
    tiles = [docs_ref[pl.ds(first // HEAD_DIM + i, 1), :] for i in range(rows // HEAD_DIM)]
    across = jnp.concatenate(tiles, axis=1)
    down = jnp.concatenate([jnp.broadcast_to(t, (HEAD_DIM, HEAD_DIM)).T for t in tiles], axis=0)
    same = jnp.concatenate([down] * (rows // HEAD_DIM), axis=1) == across
    at = lax.broadcasted_iota(jnp.int32, (rows, rows), 1)
    row = lax.broadcasted_iota(jnp.int32, (rows, rows), 0)
    bias = jnp.where(same & (at <= row), 0.0, NEG)
    sees_earlier = down == head

    def step(j, _):
        qs = heads_of(q_ref, j, count)
        ks, vs = heads_of(k_ref, j, HEADS_STEP), heads_of(v_ref, j, HEADS_STEP)
        for i in range(count):
            s = scores(qs[i], ks[i // group]) + bias
            top = jnp.max(s, axis=1, keepdims=True)
            w = jnp.exp2((s - top) * SCALE).astype(jnp.bfloat16)
            v = vs[i // group]
            both = jnp.dot(w, with_ones(v, jnp.ones_like(v)), preferred_element_type=jnp.float32)
            put_head(acc_ref, j, count, i, both[:, :HEAD_DIM])
            total_ref[j * count + i] = both[:, HEAD_DIM:]
            top_ref[j * count + i] = jnp.where(sees_earlier, jnp.broadcast_to(top, (rows, HEAD_DIM)), -NEG)
        return 0

    lax.fori_loop(0, k_ref.shape[1] // HEAD_DIM // HEADS_STEP, step, 0)


def far_kernel(choose, devices, last, group, ids, docs_ref, q_ref, acc_in, top_in, total_in, *refs):
    rows = q_ref.shape[0]
    chip, core, first, start, _ = where_am_i(ids, docs_ref, rows)
    plane, owner = chip % 4, first // rows
    places = [jnp.where((d >= 0) & (d < owner), d * rows, -(2**30)) for d in devices(plane, core, chip * ids[2])]
    if last:
        refs, (hbm, acc_out, sems) = refs[:-3], refs[-3:]
    else:
        refs, (acc_out, top_out, total_out) = refs[:-3], refs[-3:]
    count = HEADS_STEP * group
    steps = refs[0].shape[1] // HEAD_DIM // HEADS_STEP
    needed = functools.reduce(jnp.maximum, places) + rows > start

    def put(j, i, total, out, top=None):
        if last:
            out = (out / total).astype(jnp.bfloat16)
        else:
            if top is not None:
                top_out[j * count + i] = top
            total_out[j * count + i] = total
        put_head(acc_out, j, count, i, out)

    def attend(j, exact):
        qs, befores = heads_of(q_ref, j, count), heads_of(acc_in, j, count)
        tiles = [heads_of(r, j, HEADS_STEP) for r in refs]
        at = lax.broadcasted_iota(jnp.int32, (rows, HEAD_DIM), 0)
        high = None
        for h in range(HEADS_STEP):
            ks, vs = choose(plane, core, [t[h] for t in tiles])
            k = jnp.concatenate(ks, axis=0)
            ok = [jnp.where(at + place >= start, 1.0, 0.0).astype(jnp.bfloat16) for place in places]
            v = jnp.concatenate([with_ones(v, o) for v, o in zip(vs, ok)], axis=0)
            for i in range(h * group, (h + 1) * group):
                s = scores(qs[i], k)
                top, total, before = top_in[j * count + i], total_in[j * count + i], befores[i]
                if exact:
                    key = lax.broadcasted_iota(jnp.int32, (rows, rows), 1)
                    allowed = jnp.concatenate([key + place >= start for place in places], axis=1)
                    s = jnp.where(allowed, s, NEG)
                    new = jnp.maximum(top, jnp.max(s, axis=1, keepdims=True))
                    back = jnp.exp2((top - new) * SCALE)
                    top, total, before = new, total * back, before * back
                w = []
                for n in range(k.shape[0] // HEAD_DIM):
                    part = jnp.exp2((s[:, n * HEAD_DIM:(n + 1) * HEAD_DIM] - top) * SCALE).astype(jnp.bfloat16)
                    w.append(part)
                    if not exact:
                        high = part if high is None else jnp.maximum(high, part)
                both = jnp.dot(jnp.concatenate(w, axis=1), v, preferred_element_type=jnp.float32)
                put(j, i, total + both[:, HEAD_DIM:], both[:, :HEAD_DIM] + before, top if exact else None)
        return high

    def step(j, _):
        @pl.when(needed)
        def _():
            high = attend(j, False)

            @pl.when(jnp.max(high.astype(jnp.float32)) > HIGH)
            def _():
                attend(j, True)

        @pl.when(jnp.logical_not(needed))
        def _():
            for i, before in enumerate(heads_of(acc_in, j, count)):
                put(j, i, total_in[j * count + i], before)

        if last:
            part(j).start()
        return 0

    def part(j):
        width = count * HEAD_DIM
        columns = pl.ds(pl.multiple_of(j * width, width), width)
        return pltpu.make_async_copy(acc_out.at[:, columns], hbm.at[:, columns], sems.at[j])

    lax.fori_loop(0, steps, step, 0)
    if last:
        for j in range(steps):
            part(j).wait()


def pick(plane, at0, at1, at2, at3):
    return jnp.where(plane == 0, at0, jnp.where(plane == 1, at1, jnp.where(plane == 2, at2, at3)))


def choose_first(plane, core, tiles):
    mate_k, mate_v, odd_k, odd_v = tiles
    return (jnp.where(core == 1, mate_k, odd_k),), (jnp.where(core == 1, mate_v, odd_v),)


def devices_first(plane, core, base):
    return (jnp.where(core == 1, base, jnp.where(plane == 0, base - 7, -1)),)


def choose_middle(plane, core, tiles):
    def half(x1, y1, x2, y2, z2):
        pk, pv = pick(plane, x2, x2, y2, x2), pick(plane, z2, x1, y1, x1)
        qk, qv = pick(plane, y2, y2, x2, y2), pick(plane, z2, z2, z2, y1)
        return (pk, qk), (pv, qv)
    a, b = half(*tiles[:5]), half(*tiles[5:])
    return a[0] + b[0], a[1] + b[1]


def devices_middle(plane, core, base):
    p = base - 2 * pick(plane, 3, 1, 2, 1)
    q = pick(plane, -8, base - 4, base - 6, base - 4)
    return p + core, q + core, p + 1 - core, q + 1 - core


def choose_last(plane, core, tiles):
    z1, y2, x3, y3, z3 = tiles
    pk, pv = pick(plane, y2, x3, x3, x3), pick(plane, z3, y3, y3, y3)
    qk, qv = pick(plane, x3, z1, z1, z1), pick(plane, y3, z3, z3, z3)
    return (pk, qk), (pv, qv)


def devices_last(mates, plane, core, base):
    part = 1 - core if mates else core
    return base - 2 * pick(plane, 2, 3, 1, 3) + part, base - 2 * pick(plane, 1, 4, 4, 4) + part


def call(kernel, ids, docs, q, carry, pieces, keys, last=False):
    rows, width = q.shape
    steps = pieces[0].shape[1] // HEAD_DIM // HEADS_STEP
    group = width // pieces[0].shape[1]
    vmem = pl.BlockSpec(memory_space=pltpu.VMEM)
    arrays = [docs, q, *carry, *pieces]
    if last:
        out_shape = [jax.ShapeDtypeStruct(q.shape, jnp.bfloat16)]
        scratch = [pltpu.VMEM(q.shape, jnp.bfloat16), pltpu.SemaphoreType.DMA((steps,))]
    else:
        out_shape = [jax.ShapeDtypeStruct(q.shape, jnp.float32)]
        out_shape += [jax.ShapeDtypeStruct((width // HEAD_DIM, rows, HEAD_DIM), jnp.float32)] * 2
        scratch = []
    return pl.pallas_call(
        functools.partial(kernel, group),
        in_specs=[pl.BlockSpec(memory_space=pltpu.SMEM)] + [vmem] * len(arrays),
        out_specs=[pl.BlockSpec(memory_space=pl.ANY) if last else vmem] * len(out_shape),
        out_shape=out_shape,
        scratch_shapes=scratch,
        input_output_aliases={4: 1} if carry and not last else {},
        cost_estimate=pl.CostEstimate(
            flops=8 * rows * keys * width, bytes_accessed=4 * rows * width, transcendentals=0
        ),
        compiler_params=pltpu.CompilerParams(vmem_limit_bytes=VMEM_BYTES),
    )(ids, *arrays)


def shards(queries, keys, values, doc_ids):
    rows = queries.shape[0]
    chips, cores = lax.axis_size("section"), lax.axis_size("attn")
    chip, core = lax.axis_index("section"), lax.axis_index("attn")
    plane, odd_x, odd_y = chip % 4, chip % 2, (chip // 2) % 2

    def routes(target):
        return [
            (c * cores + k, at * cores + to)
            for c in range(chips) for k in range(cores) for at, to in [target(c, k)]
        ]

    def up(c):
        return (c + 4) % chips

    along = {
        "x": routes(lambda c, k: (c ^ 1, k)),
        "y": routes(lambda c, k: (c ^ 2, k)),
        "z": routes(lambda c, k: (up(c), k)),
        "mate": routes(lambda c, k: (c, 1 - k)),
        "z_odd": routes(lambda c, k: (c, k) if c % 4 == 0 and k == 0 else (up(c), k)),
        "odd": routes(lambda c, k: (c, k) if c % 4 else ((up(c), 0) if k else (c, 1))),
    }

    def send(array, way):
        return lax.ppermute(array, AXES, along[way])

    def swap(*arrays):
        return tuple(send(a, "mate") for a in arrays)

    ids = jnp.stack([chip, core, jnp.int32(cores)])
    docs = doc_ids.reshape(-1, HEAD_DIM)
    w = jnp.where

    def far(choose, devices, carry, pieces, keys, last=False):
        kernel = functools.partial(far_kernel, choose, devices, last)
        return call(kernel, ids, docs, queries, carry, pieces, keys, last)

    z1 = send(keys, "z_odd")
    x1, y1 = send(values, "x"), send(values, "y")
    odd_v = send(values, "odd")
    mate_k, mate_v = swap(keys, values)
    carry = call(own_kernel, ids, docs, queries, (), [keys, values], rows)
    z1, odd_v, *carry = barrier((z1, odd_v, *carry))
    x2 = send(w(odd_x == 0, keys, z1), "x")
    y2 = send(w(odd_y == 0, keys, z1), "y")
    z2 = send(w(plane == 1, y1, x1), "z")
    x1s, y1s, z1s = swap(x1, y1, z1)
    carry = far(choose_first, devices_first, carry, [mate_k, mate_v, z1s, odd_v], rows)
    y2, z2, y1, *carry = barrier((y2, z2, y1, *carry))
    x3 = send(y2, "x")
    y3 = send(w(odd_y == 0, x1, z2), "y")
    z3 = send(w(plane == 0, y1, values), "z")
    x2s, y2s, z2s = swap(x2, y2, z2)
    carry = far(
        choose_middle, devices_middle, carry, [x1, y1, x2, y2, z2, x1s, y1s, x2s, y2s, z2s], 4 * rows
    )
    x3, y3, z3, *carry = barrier((x3, y3, z3, *carry))
    x3s, y3s, z3s = swap(x3, y3, z3)
    carry = far(choose_last, functools.partial(devices_last, False), carry, [z1, y2, x3, y3, z3], 2 * rows)
    (out,) = far(
        choose_last, functools.partial(devices_last, True), carry, [z1s, y2s, x3s, y3s, z3s], 2 * rows, True
    )
    return out


def solution(mesh):
    split = P(AXES, None)
    return jax.shard_map(
        shards, mesh=mesh, in_specs=(split, split, split, P()), out_specs=split, check_vma=False
    )
```

time: 68.4 us -> 77.4 us (1.13); the launches traced: 68 us -> 76 us
  waiting for transfers between devices: 30.1 us -> 10.2 us
  Pallas kernels: 15.9 us -> 28.9 us
  starting transfers between devices: 9.84 us -> 18.6 us
  local copies, waits for them, and re-layouts: 6.99 us -> 11.7 us
  other arithmetic: 3.01 us -> 6.29 us
  between operations: 2.19 us -> 0.3 us
    ppermute x20 -> x21, waiting for transfers between devices: 30.1 us -> 10.2 us  [send(): return lax.ppermute(array, AXES, along[way])]
    pallas_call x4 -> x5, Pallas kernels: 15.9 us -> 28.9 us  [call(): pl.pallas_call(functools.partial(kernel, group), in_specs=[pl.BlockSpec(m...]
    ppermute x20 -> x21, starting transfers between devices: 9.84 us -> 18.6 us  [send(): return lax.ppermute(array, AXES, along[way])]
    unnamed x6 -> x18, local copies, waits for them, and re-layouts: 3.49 us -> 11.7 us
    select_n x2, other arithmetic: 1.18 us -> 4 us  [the longest x1 2.08 us: shards(): x2 = send(w(odd_x == 0, keys, z1), 'x')]
    dynamic_slice x2 -> x0, local copies, waits for them, and re-layouts: 1.54 us -> none  [the longest x1 0.78 us: shards(): window = lax.dynamic_slice_in_dim(doc_ids, low, span)]
    another operation x2 -> x0, local copies, waits for them, and re-layouts: 1.31 us -> none  [info_of(): return jnp.stack([choice, needed, start[0, 0]] + places)]
    another operation x2 -> x1, other arithmetic: 1.29 us -> 0.08 us  [shards(): ids = jnp.stack([chip, core, jnp.int32(cores)])]
  transfers between devices with their start and end apart: 20 -> 21, of which waited for: 7 -> 4; matrix products, arithmetic and copies ran while one was open for 10% -> 8% of each run, Pallas kernels for 9% -> 29%
where the time goes in v2:
time: 77.4 us; the launch traced here: 76 us
  Pallas kernels  28.9 us (37%)
  starting transfers between devices  18.6 us (24%)
  local copies, waits for them, and re-layouts  11.7 us (15%)
  waiting for transfers between devices  10.2 us (13%)
  other arithmetic  6.29 us (8%)
    pallas_call x5, Pallas kernels, call(): pl.pallas_call(functools.partial(kernel, group), in_specs=[pl.BlockSpec(m...  28.9 us
    ppermute x21, starting transfers between devices, send(): return lax.ppermute(array, AXES, along[way])  18.6 us
    unnamed x18, local copies, waits for them, and re-layouts  11.7 us
    ppermute x21, waiting for transfers between devices, send(): return lax.ppermute(array, AXES, along[way])  10.2 us
    select_n x1, other arithmetic, shards(): x2 = send(w(odd_x == 0, keys, z1), 'x')  2.08 us
    select_n x1, other arithmetic, shards(): z2 = send(w(plane == 1, y1, x1), 'z')  1.92 us
  transfers between devices with their start and end apart: 21, of which 4 were waited for; matrix products, arithmetic and copies ran while one was open for 8% of the time, Pallas kernels for 29%

profile of v2, /device:TPU:4, one launch (start us, length us, event | category | flops | bytes accessed | tf_op | source)
XLA Modules:
  0.0 76.0 jit_solution(13693269063096757700)
XLA Ops:
  0.0 3.5 %collective-permute-start = (bf16[256,1024]{1,0:T(8,128)(2,1)}, bf16[256,1024]{1,0:T(8,128)(2,1)}, u32[]{:S(2)}, u32[]{:S(2)}) collective-permute-start(bf16[256,1024]{1,0:T(8,128)(2,1)} %k_ref.1), channel_id=1, source_target_pairs={{0,0},{1,9},{2,10},{3,11},{4,12},{5,13},{6,14},{7,15},{8,8},{9,17}... | collective-permute-start | bytes 1572872 | tf_op jit(solution)/shard_map/ppermute | solution.py:251
  3.5 5.4 %collective-permute-start.1 = (bf16[256,1024]{1,0:T(8,128)(2,1)}, bf16[256,1024]{1,0:T(8,128)(2,1)}, u32[]{:S(2)}, u32[]{:S(2)}) collective-permute-start(bf16[256,1024]{1,0:T(8,128)(2,1)} %v_ref.1), channel_id=1, source_target_pairs={{0,1},{1,8},{2,2},{3,3},{4,4},{5,5},{6,6},{7,7},{8,9},{9,16},{10,1... | collective-permute-start | bytes 1572872 | tf_op jit(solution)/shard_map/ppermute | solution.py:251
  8.8 0.0 collective-permute-start.6
  8.8 1.5 %collective-permute-start.4 = (bf16[256,1024]{1,0:T(8,128)(2,1)}, bf16[256,1024]{1,0:T(8,128)(2,1)}, u32[]{:S(2)}, u32[]{:S(2)}) collective-permute-start(bf16[256,1024]{1,0:T(8,128)(2,1)} %v_ref.1), channel_id=1, source_target_pairs={{0,2},{1,3},{2,0},{3,1},{4,6},{5,7},{6,4},{7,5},{8,10},{9,11},{10,... | collective-permute-start | bytes 1572872 | tf_op jit(solution)/shard_map/ppermute | solution.py:251
  10.3 0.5 collective-permute-start.3
  10.8 0.1 pad_add_fusion.ids
  10.9 0.0 copy-start
  10.9 1.4 %copy-done = bf16[256,3072]{1,0:T(8,128)(2,1)S(1)} copy-done((bf16[256,3072]{1,0:T(8,128)(2,1)S(1)}, bf16[256,3072]{1,0:T(8,128)(2,1)}, u32[]{:S(2)}) %copy-start) | copy-done | bytes 1572888
  12.3 0.0 copy-start.6
  12.3 1.0 %copy-done.6 = bf16[256,1024]{1,0:T(8,128)(2,1)S(1)} copy-done((bf16[256,1024]{1,0:T(8,128)(2,1)S(1)}, bf16[256,1024]{1,0:T(8,128)(2,1)}, u32[]{:S(2)}) %copy-start.6) | copy-done | bytes 524312
  13.4 0.8 copy-done.7
  14.1 3.6 %shard_map.46 = (f32[256,3072]{1,0:T(8,128)S(1)}, f32[24,256,128]{2,1,0:T(8,128)S(1)}, f32[24,256,128]{2,1,0:T(8,128)S(1)}) custom-call(s32[3]{0:T(128)S(1)} %pad_add_fusion.ids, s32[64,128]{1,0:T(8,128)S(1)} %bitcast.3, bf16[256,3072]{1,0:T(8,128)(2,1)S(1)} %copy-done, bf16[256,1024]{1,0:T(8,128)(2,1)S(1)} %copy-done.6, bf16[256,1024]{1,0:T(8,128)(2,1)} %v_ref.1), custom_call_target="tpu_custom_call" | custom-call | flops 1610612736 | bytes 3145728 | tf_op jit(solution)/shard_map/pallas_call | solution.py:212
  17.8 0.0 copy-start.2
  17.8 1.6 %copy-done.2 = f32[256,3072]{1,0:T(8,128)} copy-done((f32[256,3072]{1,0:T(8,128)}, f32[256,3072]{1,0:T(8,128)S(1)}, u32[]{:S(2)}) %copy-start.2) | copy-done | bytes 3145752
  19.4 1.7 %copy-done.4 = f32[24,256,128]{2,1,0:T(8,128)} copy-done((f32[24,256,128]{2,1,0:T(8,128)}, f32[24,256,128]{2,1,0:T(8,128)S(1)}, u32[]{:S(2)}) %copy-start.4) | copy-done | bytes 3145752
  21.1 0.0 collective-permute-done.refs_0_
  21.1 0.0 collective-permute-start.7
  21.1 0.0 collective-permute-done.1.refs_3_
  21.1 0.5 collective-permute-start.8
  21.6 2.1 %broadcast_select_fusion = (bf16[256,1024]{1,0:T(8,128)(2,1)}, bf16[256,1024]{1,0:T(8,128)(2,1)}) fusion(bf16[256,1024]{1,0:T(8,128)(2,1)S(1)} %copy-done.6, bf16[256,1024]{1,0:T(8,128)(2,1)} %collective-permute-done.refs_0_, pred[]{:T(512)S(6)} %eq.20, pred[]{:T(512)S(6)} %eq.17), kind=kLoop, calls=%fused_computation | loop fusion | flops 524288 | bytes 2097154 | tf_op jit(solution)/shard_map/jit(_where)/select_n | solution.py:270
  23.7 0.0 collective-permute-done.4.refs_0_
  23.7 1.5 %collective-permute-start.2 = (bf16[256,1024]{1,0:T(8,128)(2,1)}, bf16[256,1024]{1,0:T(8,128)(2,1)}, u32[]{:S(2)}, u32[]{:S(2)}) collective-permute-start(bf16[256,1024]{1,0:T(8,128)(2,1)} %get-tuple-element.64), channel_id=1, source_target_pairs={{0,4},{1,5},{2,6},{3,7},{4,0},{5,1},{6,2},{7,3},{8,12},{9,13},{10,... | collective-permute-start | bytes 1572872 | tf_op jit(solution)/shard_map/ppermute | solution.py:251
  25.2 0.0 collective-permute-done.3.refs_1_
  25.2 1.9 %broadcast_select_fusion.2 = bf16[256,1024]{1,0:T(8,128)(2,1)} fusion(bf16[256,1024]{1,0:T(8,128)(2,1)} %collective-permute-done.3.refs_1_, bf16[256,1024]{1,0:T(8,128)(2,1)} %collective-permute-done.4.refs_0_, pred[]{:T(512)S(6)} %eq.18), kind=kLoop, calls=%fused_computation.2 | loop fusion | flops 262144 | bytes 1572865 | tf_op jit(solution)/shard_map/jit(_where)/select_n | solution.py:272
  27.1 1.6 %collective-permute-start.5 = (bf16[256,1024]{1,0:T(8,128)(2,1)}, bf16[256,1024]{1,0:T(8,128)(2,1)}, u32[]{:S(2)}, u32[]{:S(2)}) collective-permute-start(bf16[256,1024]{1,0:T(8,128)(2,1)} %broadcast_select_fusion.2), channel_id=1, source_target_pairs={{0,8},{1,9},{2,10},{3,11},{4,12},{5,13},{6,14},{7,15},{8,16},{9,17... | collective-permute-start | bytes 1572872 | tf_op jit(solution)/shard_map/ppermute | solution.py:251
  28.7 0.0 collective-permute-done.6.refs_0_
  28.7 0.5 collective-permute-start.12
  29.2 0.0 collective-permute-done.7.refs_1_
  29.2 0.0 collective-permute-start.13
  29.2 0.0 collective-permute-done.8.refs_2_.refs_0_
  29.3 0.5 collective-permute-start.14
  29.8 0.0 copy-done.8
  29.8 1.4 %copy-done.1 = bf16[256,3072]{1,0:T(8,128)(2,1)S(1)} copy-done((bf16[256,3072]{1,0:T(8,128)(2,1)S(1)}, bf16[256,3072]{1,0:T(8,128)(2,1)}, u32[]{:S(2)}) %copy-start.1) | copy-done | bytes 1572888
  31.2 1.9 %copy-done.3 = f32[256,3072]{1,0:T(8,128)S(1)} copy-done((f32[256,3072]{1,0:T(8,128)S(1)}, f32[256,3072]{1,0:T(8,128)}, u32[]{:S(2)}) %copy-start.3) | copy-done | bytes 3145752
  33.1 1.9 %copy-done.5 = f32[24,256,128]{2,1,0:T(8,128)S(1)} copy-done((f32[24,256,128]{2,1,0:T(8,128)S(1)}, f32[24,256,128]{2,1,0:T(8,128)}, u32[]{:S(2)}) %copy-start.5) | copy-done | bytes 3145752
  35.0 2.6 %shard_map.47 = (f32[256,3072]{1,0:T(8,128)S(1)}, f32[24,256,128]{2,1,0:T(8,128)S(1)}, f32[24,256,128]{2,1,0:T(8,128)S(1)}) custom-call(s32[3]{0:T(128)S(1)} %pad_add_fusion.ids, s32[64,128]{1,0:T(8,128)S(1)} %bitcast.4, bf16[256,3072]{1,0:T(8,128)(2,1)S(1)} %copy-done.1, f32[256,3072]{1,0:T(8,128)S(1)} %copy-done.3, ...), custom_call_target="tpu_custom_call", output_to_operand_aliasing={{1}: (4, {})} | custom-call | flops 1610612736 | bytes 3145728 | tf_op jit(solution)/shard_map/pallas_call | solution.py:212
  37.5 0.4 collective-permute-done.2.refs_3_.refs_1_
  37.9 5.0 %collective-permute-done.5.refs_4_ = bf16[256,1024]{1,0:T(8,128)(2,1)} collective-permute-done((bf16[256,1024]{1,0:T(8,128)(2,1)}, bf16[256,1024]{1,0:T(8,128)(2,1)}, u32[]{:S(2)}, u32[]{:S(2)}) %collective-permute-start.5) | collective-permute-done | bytes 524320 | tf_op jit(solution)/shard_map/ppermute | solution.py:251
  42.9 0.0 collective-permute-start.16
  42.9 0.5 collective-permute-start.17
  43.4 0.0 collective-permute-done.12.refs_2_
  43.4 0.0 collective-permute-start.15
  43.4 1.1 %broadcast_select_fusion.1 = bf16[256,1024]{1,0:T(8,128)(2,1)S(1)} fusion(bf16[256,1024]{1,0:T(8,128)(2,1)} %collective-permute-done.3.refs_1_, bf16[256,1024]{1,0:T(8,128)(2,1)} %v_ref.1, pred[]{:T(512)S(6)} %eq.19), kind=kLoop, calls=%fused_computation.1 | loop fusion | flops 262144 | bytes 1572865 | tf_op jit(solution)/shard_map/jit(_where)/select_n | solution.py:278
  44.5 1.1 %broadcast_select_fusion.3 = bf16[256,1024]{1,0:T(8,128)(2,1)S(1)} fusion(bf16[256,1024]{1,0:T(8,128)(2,1)} %collective-permute-done.4.refs_0_, bf16[256,1024]{1,0:T(8,128)(2,1)} %collective-permute-done.5.refs_4_, pred[]{:T(512)S(6)} %eq.17), kind=kLoop, calls=%fused_computation.3 | loop fusion | flops 262144 | bytes 1572865 | tf_op jit(solution)/shard_map/jit(_where)/select_n | solution.py:277
  45.6 0.0 collective-permute-done.13.refs_5_
  45.6 0.6 collective-permute-start.9
  46.2 0.0 collective-permute-done.14.refs_6_
  46.2 0.9 %collective-permute-start.10 = (bf16[256,1024]{1,0:T(8,128)(2,1)S(1)}, bf16[256,1024]{1,0:T(8,128)(2,1)S(1)}, u32[]{:S(2)}, u32[]{:S(2)}) collective-permute-start(bf16[256,1024]{1,0:T(8,128)(2,1)S(1)} %broadcast_select_fusion.3), channel_id=1, source_target_pairs={{0,4},{1,5},{2,6},{3,7},{4,0},{5,1},{6,2},{7,3},{8,12},{9,13},{10,... | collective-permute-start | bytes 1572872 | tf_op jit(solution)/shard_map/ppermute | solution.py:251
  47.1 0.0 collective-permute-done.16.refs_8_.refs_1_
  47.2 0.6 collective-permute-start.11
  47.7 0.0 collective-permute-done.17.refs_9_
  47.7 0.0 collective-permute-done.15.refs_7_
  47.7 10.2 %shard_map.48 = (f32[256,3072]{1,0:T(8,128)S(1)}, f32[24,256,128]{2,1,0:T(8,128)S(1)}, f32[24,256,128]{2,1,0:T(8,128)S(1)}) custom-call(s32[3]{0:T(128)S(1)} %pad_add_fusion.ids, s32[64,128]{1,0:T(8,128)S(1)} %bitcast.5, bf16[256,3072]{1,0:T(8,128)(2,1)S(1)} %copy-done.1, f32[256,3072]{1,0:T(8,128)S(1)} %get-tuple-element.48.acc_in, ...), custom_call_target="tpu_custom_call", output_to_operand_aliasing={{1}: (4, {})} | custom-call | flops 6442450944 | bytes 3145728 | tf_op jit(solution)/shard_map/pallas_call | solution.py:212
  57.9 2.4 %collective-permute-done.10.refs_3_ = bf16[256,1024]{1,0:T(8,128)(2,1)S(1)} collective-permute-done((bf16[256,1024]{1,0:T(8,128)(2,1)S(1)}, bf16[256,1024]{1,0:T(8,128)(2,1)S(1)}, u32[]{:S(2)}, u32[]{:S(2)}) %collective-permute-start.10) | collective-permute-done | bytes 524320 | tf_op jit(solution)/shard_map/ppermute | solution.py:251
  60.3 2.4 %collective-permute-done.11.refs_4_ = bf16[256,1024]{1,0:T(8,128)(2,1)S(1)} collective-permute-done((bf16[256,1024]{1,0:T(8,128)(2,1)S(1)}, bf16[256,1024]{1,0:T(8,128)(2,1)S(1)}, u32[]{:S(2)}, u32[]{:S(2)}) %collective-permute-start.11) | collective-permute-done | bytes 524320 | tf_op jit(solution)/shard_map/ppermute | solution.py:251
  62.7 0.0 collective-permute-done.9.refs_2_
  62.7 0.0 collective-permute-start.18
  62.7 0.5 collective-permute-start.19
  63.2 0.0 collective-permute-start.20
  63.2 6.0 %shard_map.49 = (f32[256,3072]{1,0:T(8,128)S(1)}, f32[24,256,128]{2,1,0:T(8,128)S(1)}, f32[24,256,128]{2,1,0:T(8,128)S(1)}) custom-call(s32[3]{0:T(128)S(1)} %pad_add_fusion.ids, s32[64,128]{1,0:T(8,128)S(1)} %bitcast.6, bf16[256,3072]{1,0:T(8,128)(2,1)S(1)} %copy-done.1, f32[256,3072]{1,0:T(8,128)S(1)} %get-tuple-element.54.acc_in, ...), custom_call_target="tpu_custom_call", output_to_operand_aliasing={{1}: (4, {})} | custom-call | flops 3221225472 | bytes 3145728 | tf_op jit(solution)/shard_map/pallas_call | solution.py:212
  69.3 0.0 collective-permute-done.18.refs_2_
  69.3 0.0 collective-permute-done.19.refs_3_
  69.3 0.0 collective-permute-done.20.refs_4_
  69.3 6.5 %shard_map.50 = bf16[256,3072]{1,0:T(8,128)(2,1)} custom-call(s32[3]{0:T(128)S(1)} %pad_add_fusion.ids, s32[64,128]{1,0:T(8,128)S(1)} %bitcast.7, bf16[256,3072]{1,0:T(8,128)(2,1)S(1)} %copy-done.1, f32[256,3072]{1,0:T(8,128)S(1)} %get-tuple-element.60.acc_in, f32[24,256,128]{2,1,0:T(8,128)S(1)} %get-tuple-element.61.top_in, ...), custom_call_target="tpu_custom_call" | custom-call | flops 3221225472 | bytes 3145728 | tf_op jit(solution)/shard_map/pallas_call | solution.py:212
  (6 shorter events, 0.0 us)
Async XLA Ops:
  0.0 21.1 %collective-permute-start = (bf16[256,1024]{1,0:T(8,128)(2,1)}, bf16[256,1024]{1,0:T(8,128)(2,1)}, u32[]{:S(2)}, u32[]{:S(2)}) collective-permute-start(bf16[256,1024]{1,0:T(8,128)(2,1)} %k_ref.1), channel_id=1, source_target_pairs={{0,0},{1,9},{2,10},{3,11},{4,12},{5,13},{6,14},{7,15},{8,8},{9,17}... | collective-permute-start | bytes 1572872 | tf_op jit(solution)/shard_map/ppermute | solution.py:251
  3.5 17.6 %collective-permute-start.1 = (bf16[256,1024]{1,0:T(8,128)(2,1)}, bf16[256,1024]{1,0:T(8,128)(2,1)}, u32[]{:S(2)}, u32[]{:S(2)}) collective-permute-start(bf16[256,1024]{1,0:T(8,128)(2,1)} %v_ref.1), channel_id=1, source_target_pairs={{0,1},{1,8},{2,2},{3,3},{4,4},{5,5},{6,6},{7,7},{8,9},{9,16},{10,1... | collective-permute-start | bytes 1572872 | tf_op jit(solution)/shard_map/ppermute | solution.py:251
  8.8 19.9 %collective-permute-start.6 = (bf16[256,1024]{1,0:T(8,128)(2,1)}, bf16[256,1024]{1,0:T(8,128)(2,1)}, u32[]{:S(2)}, u32[]{:S(2)}) collective-permute-start(bf16[256,1024]{1,0:T(8,128)(2,1)} %k_ref.1), channel_id=1, source_target_pairs={{0,1},{1,0},{2,3},{3,2},{4,5},{5,4},{6,7},{7,6},{8,9},{9,8},{10,11... | collective-permute-start | bytes 1572872 | tf_op jit(solution)/shard_map/ppermute | solution.py:251
  8.8 14.8 %collective-permute-start.4 = (bf16[256,1024]{1,0:T(8,128)(2,1)}, bf16[256,1024]{1,0:T(8,128)(2,1)}, u32[]{:S(2)}, u32[]{:S(2)}) collective-permute-start(bf16[256,1024]{1,0:T(8,128)(2,1)} %v_ref.1), channel_id=1, source_target_pairs={{0,2},{1,3},{2,0},{3,1},{4,6},{5,7},{6,4},{7,5},{8,10},{9,11},{10,... | collective-permute-start | bytes 1572872 | tf_op jit(solution)/shard_map/ppermute | solution.py:251
  10.3 14.9 %collective-permute-start.3 = (bf16[256,1024]{1,0:T(8,128)(2,1)}, bf16[256,1024]{1,0:T(8,128)(2,1)}, u32[]{:S(2)}, u32[]{:S(2)}) collective-permute-start(bf16[256,1024]{1,0:T(8,128)(2,1)} %v_ref.1), channel_id=1, source_target_pairs={{0,4},{1,5},{2,6},{3,7},{4,0},{5,1},{6,2},{7,3},{8,12},{9,13},{10,... | collective-permute-start | bytes 1572872 | tf_op jit(solution)/shard_map/ppermute | solution.py:251
  10.9 1.4 %copy-start = (bf16[256,3072]{1,0:T(8,128)(2,1)S(1)}, bf16[256,3072]{1,0:T(8,128)(2,1)}, u32[]{:S(2)}) copy-start(bf16[256,3072]{1,0:T(8,128)(2,1)} %q_ref.9) | copy-start | bytes 4718596
  12.3 1.0 %copy-start.6 = (bf16[256,1024]{1,0:T(8,128)(2,1)S(1)}, bf16[256,1024]{1,0:T(8,128)(2,1)}, u32[]{:S(2)}) copy-start(bf16[256,1024]{1,0:T(8,128)(2,1)} %k_ref.1) | copy-start | bytes 1572868
  13.4 0.8 copy-start.7
  17.8 1.6 %copy-start.2 = (f32[256,3072]{1,0:T(8,128)}, f32[256,3072]{1,0:T(8,128)S(1)}, u32[]{:S(2)}) copy-start(f32[256,3072]{1,0:T(8,128)S(1)} %get-tuple-element.38.acc_in) | copy-start | bytes 9437188
  19.4 1.7 %copy-start.4 = (f32[24,256,128]{2,1,0:T(8,128)}, f32[24,256,128]{2,1,0:T(8,128)S(1)}, u32[]{:S(2)}) copy-start(f32[24,256,128]{2,1,0:T(8,128)S(1)} %get-tuple-element.40.total_in) | copy-start | bytes 9437188
  21.1 8.7 %copy-start.8 = (s32[8192]{0:T(1024)S(1)}, s32[8192]{0:T(1024)}, u32[]{:S(2)}) copy-start(s32[8192]{0:T(1024)} %param.7) | copy-start | bytes 98308
  21.1 8.2 %collective-permute-start.7 = (bf16[256,1024]{1,0:T(8,128)(2,1)}, bf16[256,1024]{1,0:T(8,128)(2,1)}, u32[]{:S(2)}, u32[]{:S(2)}) collective-permute-start(bf16[256,1024]{1,0:T(8,128)(2,1)} %v_ref.1), channel_id=1, source_target_pairs={{0,1},{1,0},{2,3},{3,2},{4,5},{5,4},{6,7},{7,6},{8,9},{9,8},{10,11... | collective-permute-start | bytes 1572872 | tf_op jit(solution)/shard_map/ppermute | solution.py:251
  21.1 8.1 %collective-permute-start.8 = (bf16[256,1024]{1,0:T(8,128)(2,1)}, bf16[256,1024]{1,0:T(8,128)(2,1)}, u32[]{:S(2)}, u32[]{:S(2)}) collective-permute-start(bf16[256,1024]{1,0:T(8,128)(2,1)} %collective-permute-done.refs_0_), channel_id=1, source_target_pairs={{0,1},{1,0},{2,3},{3,2},{4,5},{5,4},{6,7},{7,6},{8,9},{9,8},{10,11... | collective-permute-start | bytes 1572872 | tf_op jit(solution)/shard_map/ppermute | solution.py:251
  23.7 14.2 %collective-permute-start.2 = (bf16[256,1024]{1,0:T(8,128)(2,1)}, bf16[256,1024]{1,0:T(8,128)(2,1)}, u32[]{:S(2)}, u32[]{:S(2)}) collective-permute-start(bf16[256,1024]{1,0:T(8,128)(2,1)} %get-tuple-element.64), channel_id=1, source_target_pairs={{0,4},{1,5},{2,6},{3,7},{4,0},{5,1},{6,2},{7,3},{8,12},{9,13},{10,... | collective-permute-start | bytes 1572872 | tf_op jit(solution)/shard_map/ppermute | solution.py:251
  27.1 15.7 %collective-permute-start.5 = (bf16[256,1024]{1,0:T(8,128)(2,1)}, bf16[256,1024]{1,0:T(8,128)(2,1)}, u32[]{:S(2)}, u32[]{:S(2)}) collective-permute-start(bf16[256,1024]{1,0:T(8,128)(2,1)} %broadcast_select_fusion.2), channel_id=1, source_target_pairs={{0,8},{1,9},{2,10},{3,11},{4,12},{5,13},{6,14},{7,15},{8,16},{9,17... | collective-permute-start | bytes 1572872 | tf_op jit(solution)/shard_map/ppermute | solution.py:251
  28.7 14.7 %collective-permute-start.12 = (bf16[256,1024]{1,0:T(8,128)(2,1)}, bf16[256,1024]{1,0:T(8,128)(2,1)}, u32[]{:S(2)}, u32[]{:S(2)}) collective-permute-start(bf16[256,1024]{1,0:T(8,128)(2,1)} %get-tuple-element.63), channel_id=1, source_target_pairs={{0,2},{1,3},{2,0},{3,1},{4,6},{5,7},{6,4},{7,5},{8,10},{9,11},{10,... | collective-permute-start | bytes 1572872 | tf_op jit(solution)/shard_map/ppermute | solution.py:251
  29.2 16.4 %collective-permute-start.13 = (bf16[256,1024]{1,0:T(8,128)(2,1)}, bf16[256,1024]{1,0:T(8,128)(2,1)S(1)}, u32[]{:S(2)}, u32[]{:S(2)}) collective-permute-start(bf16[256,1024]{1,0:T(8,128)(2,1)} %collective-permute-done.4.refs_0_), channel_id=1, source_target_pairs={{0,1},{1,0},{2,3},{3,2},{4,5},{5,4},{6,7},{7,6},{8,9},{9,8},{10,11... | collective-permute-start | bytes 1572872 | tf_op jit(solution)/shard_map/ppermute | solution.py:251
  29.3 17.0 %collective-permute-start.14 = (bf16[256,1024]{1,0:T(8,128)(2,1)}, bf16[256,1024]{1,0:T(8,128)(2,1)S(1)}, u32[]{:S(2)}, u32[]{:S(2)}) collective-permute-start(bf16[256,1024]{1,0:T(8,128)(2,1)} %collective-permute-done.3.refs_1_), channel_id=1, source_target_pairs={{0,1},{1,0},{2,3},{3,2},{4,5},{5,4},{6,7},{7,6},{8,9},{9,8},{10,11... | collective-permute-start | bytes 1572872 | tf_op jit(solution)/shard_map/ppermute | solution.py:251
  29.8 1.4 %copy-start.1 = (bf16[256,3072]{1,0:T(8,128)(2,1)S(1)}, bf16[256,3072]{1,0:T(8,128)(2,1)}, u32[]{:S(2)}) copy-start(bf16[256,3072]{1,0:T(8,128)(2,1)} %q_ref.9) | copy-start | bytes 4718596
  31.2 1.9 %copy-start.3 = (f32[256,3072]{1,0:T(8,128)S(1)}, f32[256,3072]{1,0:T(8,128)}, u32[]{:S(2)}) copy-start(f32[256,3072]{1,0:T(8,128)} %copy-done.2) | copy-start | bytes 9437188
  33.1 1.9 %copy-start.5 = (f32[24,256,128]{2,1,0:T(8,128)S(1)}, f32[24,256,128]{2,1,0:T(8,128)}, u32[]{:S(2)}) copy-start(f32[24,256,128]{2,1,0:T(8,128)} %copy-done.4) | copy-start | bytes 9437188
  42.9 4.3 %collective-permute-start.16 = (bf16[256,1024]{1,0:T(8,128)(2,1)}, bf16[256,1024]{1,0:T(8,128)(2,1)S(1)}, u32[]{:S(2)}, u32[]{:S(2)}) collective-permute-start(bf16[256,1024]{1,0:T(8,128)(2,1)} %collective-permute-done.2.refs_3_.refs_1_), channel_id=1, source_target_pairs={{0,1},{1,0},{2,3},{3,2},{4,5},{5,4},{6,7},{7,6},{8,9},{9,8},{10,11... | collective-permute-start | bytes 1572872 | tf_op jit(solution)/shard_map/ppermute | solution.py:251
  42.9 4.8 %collective-permute-start.17 = (bf16[256,1024]{1,0:T(8,128)(2,1)}, bf16[256,1024]{1,0:T(8,128)(2,1)S(1)}, u32[]{:S(2)}, u32[]{:S(2)}) collective-permute-start(bf16[256,1024]{1,0:T(8,128)(2,1)} %collective-permute-done.5.refs_4_), channel_id=1, source_target_pairs={{0,1},{1,0},{2,3},{3,2},{4,5},{5,4},{6,7},{7,6},{8,9},{9,8},{10,11... | collective-permute-start | bytes 1572872 | tf_op jit(solution)/shard_map/ppermute | solution.py:251
  43.4 4.3 %collective-permute-start.15 = (bf16[256,1024]{1,0:T(8,128)(2,1)}, bf16[256,1024]{1,0:T(8,128)(2,1)S(1)}, u32[]{:S(2)}, u32[]{:S(2)}) collective-permute-start(bf16[256,1024]{1,0:T(8,128)(2,1)} %collective-permute-done.12.refs_2_), channel_id=1, source_target_pairs={{0,1},{1,0},{2,3},{3,2},{4,5},{5,4},{6,7},{7,6},{8,9},{9,8},{10,11... | collective-permute-start | bytes 1572872 | tf_op jit(solution)/shard_map/ppermute | solution.py:251
  45.6 17.1 %collective-permute-start.9 = (bf16[256,1024]{1,0:T(8,128)(2,1)}, bf16[256,1024]{1,0:T(8,128)(2,1)S(1)}, u32[]{:S(2)}, u32[]{:S(2)}) collective-permute-start(bf16[256,1024]{1,0:T(8,128)(2,1)} %collective-permute-done.2.refs_3_.refs_1_), channel_id=1, source_target_pairs={{0,2},{1,3},{2,0},{3,1},{4,6},{5,7},{6,4},{7,5},{8,10},{9,11},{10,... | collective-permute-start | bytes 1572872 | tf_op jit(solution)/shard_map/ppermute | solution.py:251
  46.2 14.1 %collective-permute-start.10 = (bf16[256,1024]{1,0:T(8,128)(2,1)S(1)}, bf16[256,1024]{1,0:T(8,128)(2,1)S(1)}, u32[]{:S(2)}, u32[]{:S(2)}) collective-permute-start(bf16[256,1024]{1,0:T(8,128)(2,1)S(1)} %broadcast_select_fusion.3), channel_id=1, source_target_pairs={{0,4},{1,5},{2,6},{3,7},{4,0},{5,1},{6,2},{7,3},{8,12},{9,13},{10,... | collective-permute-start | bytes 1572872 | tf_op jit(solution)/shard_map/ppermute | solution.py:251
  47.2 15.6 %collective-permute-start.11 = (bf16[256,1024]{1,0:T(8,128)(2,1)S(1)}, bf16[256,1024]{1,0:T(8,128)(2,1)S(1)}, u32[]{:S(2)}, u32[]{:S(2)}) collective-permute-start(bf16[256,1024]{1,0:T(8,128)(2,1)S(1)} %broadcast_select_fusion.1), channel_id=1, source_target_pairs={{0,8},{1,9},{2,10},{3,11},{4,12},{5,13},{6,14},{7,15},{8,16},{9,17... | collective-permute-start | bytes 1572872 | tf_op jit(solution)/shard_map/ppermute | solution.py:251
  62.7 6.6 %collective-permute-start.18 = (bf16[256,1024]{1,0:T(8,128)(2,1)S(1)}, bf16[256,1024]{1,0:T(8,128)(2,1)S(1)}, u32[]{:S(2)}, u32[]{:S(2)}) collective-permute-start(bf16[256,1024]{1,0:T(8,128)(2,1)S(1)} %collective-permute-done.9.refs_2_), channel_id=1, source_target_pairs={{0,1},{1,0},{2,3},{3,2},{4,5},{5,4},{6,7},{7,6},{8,9},{9,8},{10,11... | collective-permute-start | bytes 1572872 | tf_op jit(solution)/shard_map/ppermute | solution.py:251
  62.7 6.6 %collective-permute-start.19 = (bf16[256,1024]{1,0:T(8,128)(2,1)S(1)}, bf16[256,1024]{1,0:T(8,128)(2,1)S(1)}, u32[]{:S(2)}, u32[]{:S(2)}) collective-permute-start(bf16[256,1024]{1,0:T(8,128)(2,1)S(1)} %collective-permute-done.10.refs_3_), channel_id=1, source_target_pairs={{0,1},{1,0},{2,3},{3,2},{4,5},{5,4},{6,7},{7,6},{8,9},{9,8},{10,11... | collective-permute-start | bytes 1572872 | tf_op jit(solution)/shard_map/ppermute | solution.py:251
  63.2 6.1 %collective-permute-start.20 = (bf16[256,1024]{1,0:T(8,128)(2,1)S(1)}, bf16[256,1024]{1,0:T(8,128)(2,1)S(1)}, u32[]{:S(2)}, u32[]{:S(2)}) collective-permute-start(bf16[256,1024]{1,0:T(8,128)(2,1)S(1)} %collective-permute-done.11.refs_4_), channel_id=1, source_target_pairs={{0,1},{1,0},{2,3},{3,2},{4,5},{5,4},{6,7},{7,6},{8,9},{9,8},{10,11... | collective-permute-start | bytes 1572872 | tf_op jit(solution)/shard_map/ppermute | solution.py:251

commit v3 on v2

--- a/solution.py
+++ b/solution.py
@@ -243,8 +243,6 @@
         "y": routes(lambda c, k: (c ^ 2, k)),
         "z": routes(lambda c, k: (up(c), k)),
         "mate": routes(lambda c, k: (c, 1 - k)),
-        "z_odd": routes(lambda c, k: (c, k) if c % 4 == 0 and k == 0 else (up(c), k)),
-        "odd": routes(lambda c, k: (c, k) if c % 4 else ((up(c), 0) if k else (c, 1))),
     }
 
     def send(array, way):
@@ -261,21 +259,22 @@
         kernel = functools.partial(far_kernel, choose, devices, last)
         return call(kernel, ids, docs, queries, carry, pieces, keys, last)
 
-    z1 = send(keys, "z_odd")
+    mate_v = send(values, "mate")
     x1, y1 = send(values, "x"), send(values, "y")
-    odd_v = send(values, "odd")
-    mate_k, mate_v = swap(keys, values)
-    carry = call(own_kernel, ids, docs, queries, (), [keys, values], rows)
-    z1, odd_v, *carry = barrier((z1, odd_v, *carry))
+    z1 = send(w((plane == 0) & (core == 0), mate_v, keys), "z")
+    mate_k = send(keys, "mate")
+    x1, y1 = barrier((x1, y1))
+    up2 = w(plane == 1, y1, x1)
+    z2 = send(up2, "z")
+    z1, up2, mate_k, mate_v = barrier((z1, up2, mate_k, mate_v))
     x2 = send(w(odd_x == 0, keys, z1), "x")
     y2 = send(w(odd_y == 0, keys, z1), "y")
-    z2 = send(w(plane == 1, y1, x1), "z")
     x1s, y1s, z1s = swap(x1, y1, z1)
-    carry = far(choose_first, devices_first, carry, [mate_k, mate_v, z1s, odd_v], rows)
+    carry = call(own_kernel, ids, docs, queries, (), [keys, values], rows)
+    carry = far(choose_first, devices_first, carry, [mate_k, mate_v, z1s, z1], rows)
     y2, z2, y1, *carry = barrier((y2, z2, y1, *carry))
-    x3 = send(y2, "x")
-    y3 = send(w(odd_y == 0, x1, z2), "y")
-    z3 = send(w(plane == 0, y1, values), "z")
+    up3, side3 = w(plane == 0, y1, values), w(odd_y == 0, x1, z2)
+    z3, x3, y3 = send(up3, "z"), send(y2, "x"), send(side3, "y")
     x2s, y2s, z2s = swap(x2, y2, z2)
     carry = far(
         choose_middle, devices_middle, carry, [x1, y1, x2, y2, z2, x1s, y1s, x2s, y2s, z2s], 4 * rows

time: 77.4 us -> 66.8 us (0.86); the launches traced: 76 us -> 67.4 us
  waiting for transfers between devices: 10.2 us -> 26 us
  local copies, waits for them, and re-layouts: 11.7 us -> 0.01 us
  starting transfers between devices: 18.6 us -> 11.8 us
  other arithmetic: 6.29 us -> 3.28 us
  Pallas kernels: 28.9 us -> 26 us
    ppermute x21 -> x20, waiting for transfers between devices: 10.2 us -> 26 us  [send(): return lax.ppermute(array, AXES, along[way])]
    unnamed x18 -> x8, local copies, waits for them, and re-layouts: 11.7 us -> 0.01 us
    ppermute x21 -> x20, starting transfers between devices: 18.6 us -> 11.8 us  [send(): return lax.ppermute(array, AXES, along[way])]
    pallas_call x5, Pallas kernels: 28.9 us -> 26 us  [call(): pl.pallas_call(functools.partial(kernel, group), in_specs=[pl.BlockSpec(m...]
    select_n x3 -> x4, other arithmetic: 4.13 us -> 2.09 us  [the longest x1 1.89 us: shards(): z1 = send(w((plane == 0) & (core == 0), mate_v, keys), 'z')]
    select_n x1, other arithmetic: 2.08 us -> 1.11 us  [shards(): x2 = send(w(odd_x == 0, keys, z1), 'x')]
  transfers between devices with their start and end apart: 21 -> 20, of which waited for: 4 -> 7; matrix products, arithmetic and copies ran while one was open for 8% -> 5% of each run, Pallas kernels for 29% -> 30%
where the time goes in v3:
time: 66.8 us; the launch traced here: 67.4 us
  waiting for transfers between devices  26 us (39%)
  Pallas kernels  26 us (39%)
  starting transfers between devices  11.8 us (18%)
  other arithmetic  3.28 us (5%)
    pallas_call x5, Pallas kernels, call(): pl.pallas_call(functools.partial(kernel, group), in_specs=[pl.BlockSpec(m...  26 us
    ppermute x20, waiting for transfers between devices, send(): return lax.ppermute(array, AXES, along[way])  26 us
    ppermute x20, starting transfers between devices, send(): return lax.ppermute(array, AXES, along[way])  11.8 us
    select_n x1, other arithmetic, shards(): z1 = send(w((plane == 0) & (core == 0), mate_v, keys), 'z')  1.89 us
  transfers between devices with their start and end apart: 20, of which 7 were waited for; matrix products, arithmetic and copies ran while one was open for 5% of the time, Pallas kernels for 30%

profile of v3, /device:TPU:4, one launch (start us, length us, event | category | flops | bytes accessed | tf_op | source)
XLA Modules:
  0.0 67.4 jit_solution(15636442260978978319)
XLA Ops:
  0.0 0.0 copy-start.3
  0.0 0.0 copy-start
  0.0 0.0 collective-permute-start
  0.0 1.6 %collective-permute-start.2 = (bf16[256,1024]{1,0:T(8,128)(2,1)}, bf16[256,1024]{1,0:T(8,128)(2,1)S(1)}, u32[]{:S(2)}, u32[]{:S(2)}) collective-permute-start(bf16[256,1024]{1,0:T(8,128)(2,1)} %v_ref.1), channel_id=1, source_target_pairs={{0,2},{1,3},{2,0},{3,1},{4,6},{5,7},{6,4},{7,5},{8,10},{9,11},{10,... | collective-permute-start | bytes 1572872 | tf_op jit(solution)/shard_map/ppermute | solution.py:249
  1.6 0.5 collective-permute-start.3
  2.1 0.0 collective-permute-start.4
  2.1 0.0 collective-permute-done.refs_1_
  2.1 1.9 %broadcast_select_fusion.3 = bf16[256,1024]{1,0:T(8,128)(2,1)} fusion(bf16[256,1024]{1,0:T(8,128)(2,1)S(1)} %collective-permute-done.refs_1_, bf16[256,1024]{1,0:T(8,128)(2,1)} %k_ref.1, pred[]{:T(512)S(6)} %and.26), kind=kLoop, calls=%fused_computation.3 | loop fusion | flops 262144 | bytes 1572865 | tf_op jit(solution)/shard_map/jit(_where)/select_n | solution.py:264
  4.0 1.6 %collective-permute-start.1 = (bf16[256,1024]{1,0:T(8,128)(2,1)}, bf16[256,1024]{1,0:T(8,128)(2,1)S(1)}, u32[]{:S(2)}, u32[]{:S(2)}) collective-permute-start(bf16[256,1024]{1,0:T(8,128)(2,1)} %broadcast_select_fusion.3), channel_id=1, source_target_pairs={{0,8},{1,9},{2,10},{3,11},{4,12},{5,13},{6,14},{7,15},{8,16},{9,17... | collective-permute-start | bytes 1572872 | tf_op jit(solution)/shard_map/ppermute | solution.py:249
  5.6 0.0 copy-start.1
  5.6 0.0 copy-start.2
  5.6 9.0 %collective-permute-done.2.refs_0_ = bf16[256,1024]{1,0:T(8,128)(2,1)S(1)} collective-permute-done((bf16[256,1024]{1,0:T(8,128)(2,1)}, bf16[256,1024]{1,0:T(8,128)(2,1)S(1)}, u32[]{:S(2)}, u32[]{:S(2)}) %collective-permute-start.2) | collective-permute-done | bytes 524320 | tf_op jit(solution)/shard_map/ppermute | solution.py:249
  14.6 1.3 %collective-permute-done.3.refs_1_ = bf16[256,1024]{1,0:T(8,128)(2,1)} collective-permute-done((bf16[256,1024]{1,0:T(8,128)(2,1)}, bf16[256,1024]{1,0:T(8,128)(2,1)}, u32[]{:S(2)}, u32[]{:S(2)}) %collective-permute-start.3) | collective-permute-done | bytes 524320 | tf_op jit(solution)/shard_map/ppermute | solution.py:249
  15.9 0.1 broadcast_select_fusion.2
  15.9 1.6 %collective-permute-start.6 = (bf16[256,1024]{1,0:T(8,128)(2,1)S(1)}, bf16[256,1024]{1,0:T(8,128)(2,1)S(1)}, u32[]{:S(2)}, u32[]{:S(2)}) collective-permute-start(bf16[256,1024]{1,0:T(8,128)(2,1)S(1)} %broadcast_select_fusion.2), channel_id=1, source_target_pairs={{0,8},{1,9},{2,10},{3,11},{4,12},{5,13},{6,14},{7,15},{8,16},{9,17... | collective-permute-start | bytes 1572872 | tf_op jit(solution)/shard_map/ppermute | solution.py:249
  17.6 0.0 collective-permute-done.4.refs_0_
  17.6 3.2 %collective-permute-done.1.refs_3_.refs_0_ = bf16[256,1024]{1,0:T(8,128)(2,1)S(1)} collective-permute-done((bf16[256,1024]{1,0:T(8,128)(2,1)}, bf16[256,1024]{1,0:T(8,128)(2,1)S(1)}, u32[]{:S(2)}, u32[]{:S(2)}) %collective-permute-start.1) | collective-permute-done | bytes 524320 | tf_op jit(solution)/shard_map/ppermute | solution.py:249
  20.7 0.0 collective-permute-start.7
  20.7 1.1 %broadcast_select_fusion = (bf16[256,1024]{1,0:T(8,128)(2,1)S(1)}, bf16[256,1024]{1,0:T(8,128)(2,1)S(1)}) fusion(bf16[256,1024]{1,0:T(8,128)(2,1)} %k_ref.1, bf16[256,1024]{1,0:T(8,128)(2,1)S(1)} %collective-permute-done.1.refs_3_.refs_0_, pred[]{:T(512)S(6)} %eq.25, pred[]{:T(512)S(6)} %eq.21), kind=kLoop, calls=%fused_computation | loop fusion | flops 524288 | bytes 2097154 | tf_op jit(solution)/shard_map/jit(_where)/select_n | solution.py:270
  21.9 0.4 collective-permute-start.5
  22.3 1.7 %collective-permute-start.11 = (bf16[256,1024]{1,0:T(8,128)(2,1)S(1)}, bf16[256,1024]{1,0:T(8,128)(2,1)S(1)}, u32[]{:S(2)}, u32[]{:S(2)}) collective-permute-start(bf16[256,1024]{1,0:T(8,128)(2,1)S(1)} %get-tuple-element.63), channel_id=1, source_target_pairs={{0,2},{1,3},{2,0},{3,1},{4,6},{5,7},{6,4},{7,5},{8,10},{9,11},{10,... | collective-permute-start | bytes 1572872 | tf_op jit(solution)/shard_map/ppermute | solution.py:249
  23.9 0.1 pad_add_fusion.ids
  24.0 0.0 copy-done.3
  24.0 0.0 copy-done
  24.0 0.0 copy-done.1
  24.0 0.0 copy-done.2
  24.0 3.1 %shard_map.46 = (f32[256,3072]{1,0:T(8,128)S(1)}, f32[24,256,128]{2,1,0:T(8,128)S(1)}, f32[24,256,128]{2,1,0:T(8,128)S(1)}) custom-call(s32[3]{0:T(128)S(1)} %pad_add_fusion.ids, s32[64,128]{1,0:T(8,128)S(1)} %bitcast.3, bf16[256,3072]{1,0:T(8,128)(2,1)S(1)} %copy-done, bf16[256,1024]{1,0:T(8,128)(2,1)S(1)} %copy-done.1, bf16[256,1024]{1,0:T(8,128)(2,1)S(1)} %copy-done.2), custom_call_target="tpu_custom_call" | custom-call | flops 1610612736 | bytes 3145728 | tf_op jit(solution)/shard_map/pallas_call | solution.py:212
  27.2 0.1 collective-permute-start.12
  27.2 0.0 collective-permute-done.7.refs_2_.refs_0_
  27.2 0.5 collective-permute-start.13
  27.7 2.1 %shard_map.47 = (f32[256,3072]{1,0:T(8,128)S(1)}, f32[24,256,128]{2,1,0:T(8,128)S(1)}, f32[24,256,128]{2,1,0:T(8,128)S(1)}) custom-call(s32[3]{0:T(128)S(1)} %pad_add_fusion.ids, s32[64,128]{1,0:T(8,128)S(1)} %bitcast.4, bf16[256,3072]{1,0:T(8,128)(2,1)S(1)} %copy-done, f32[256,3072]{1,0:T(8,128)S(1)} %get-tuple-element.37.acc_in, ...), custom_call_target="tpu_custom_call", output_to_operand_aliasing={{1}: (4, {})} | custom-call | flops 1610612736 | bytes 3145728 | tf_op jit(solution)/shard_map/pallas_call | solution.py:212
  29.8 1.8 %collective-permute-done.6.refs_4_ = bf16[256,1024]{1,0:T(8,128)(2,1)S(1)} collective-permute-done((bf16[256,1024]{1,0:T(8,128)(2,1)S(1)}, bf16[256,1024]{1,0:T(8,128)(2,1)S(1)}, u32[]{:S(2)}, u32[]{:S(2)}) %collective-permute-start.6) | collective-permute-done | bytes 524320 | tf_op jit(solution)/shard_map/ppermute | solution.py:249
  31.6 4.6 %collective-permute-done.5.refs_3_.refs_1_ = bf16[256,1024]{1,0:T(8,128)(2,1)S(1)} collective-permute-done((bf16[256,1024]{1,0:T(8,128)(2,1)S(1)}, bf16[256,1024]{1,0:T(8,128)(2,1)S(1)}, u32[]{:S(2)}, u32[]{:S(2)}) %collective-permute-start.5) | collective-permute-done | bytes 524320 | tf_op jit(solution)/shard_map/ppermute | solution.py:249
  36.3 0.0 collective-permute-start.15
  36.3 0.5 collective-permute-start.16
  36.8 0.0 collective-permute-done.11.refs_2_
  36.8 0.0 collective-permute-start.14
  36.8 0.1 broadcast_select_fusion.4
  36.8 0.1 broadcast_select_fusion.1
  36.9 0.0 collective-permute-done.12.refs_5_
  36.9 1.6 %collective-permute-start.8 = (bf16[256,1024]{1,0:T(8,128)(2,1)S(1)}, bf16[256,1024]{1,0:T(8,128)(2,1)S(1)}, u32[]{:S(2)}, u32[]{:S(2)}) collective-permute-start(bf16[256,1024]{1,0:T(8,128)(2,1)S(1)} %collective-permute-done.5.refs_3_.refs_1_), channel_id=1, source_target_pairs={{0,2},{1,3},{2,0},{3,1},{4,6},{5,7},{6,4},{7,5},{8,10},{9,11},{10,... | collective-permute-start | bytes 1572872 | tf_op jit(solution)/shard_map/ppermute | solution.py:249
  38.5 0.0 collective-permute-done.13.refs_6_
  38.5 1.2 %collective-permute-start.9 = (bf16[256,1024]{1,0:T(8,128)(2,1)S(1)}, bf16[256,1024]{1,0:T(8,128)(2,1)S(1)}, u32[]{:S(2)}, u32[]{:S(2)}) collective-permute-start(bf16[256,1024]{1,0:T(8,128)(2,1)S(1)} %broadcast_select_fusion.4), channel_id=1, source_target_pairs={{0,4},{1,5},{2,6},{3,7},{4,0},{5,1},{6,2},{7,3},{8,12},{9,13},{10,... | collective-permute-start | bytes 1572872 | tf_op jit(solution)/shard_map/ppermute | solution.py:249
  39.8 0.0 collective-permute-done.15.refs_8_.refs_1_
  39.8 0.0 collective-permute-start.10
  39.8 0.0 collective-permute-done.16.refs_9_
  39.8 0.0 collective-permute-done.14.refs_7_
  39.8 9.5 %shard_map.48 = (f32[256,3072]{1,0:T(8,128)S(1)}, f32[24,256,128]{2,1,0:T(8,128)S(1)}, f32[24,256,128]{2,1,0:T(8,128)S(1)}) custom-call(s32[3]{0:T(128)S(1)} %pad_add_fusion.ids, s32[64,128]{1,0:T(8,128)S(1)} %bitcast.5, bf16[256,3072]{1,0:T(8,128)(2,1)S(1)} %copy-done, f32[256,3072]{1,0:T(8,128)S(1)} %get-tuple-element.48.acc_in, ...), custom_call_target="tpu_custom_call", output_to_operand_aliasing={{1}: (4, {})} | custom-call | flops 6442450944 | bytes 3145728 | tf_op jit(solution)/shard_map/pallas_call | solution.py:212
  49.3 3.3 %collective-permute-done.9.refs_3_ = bf16[256,1024]{1,0:T(8,128)(2,1)S(1)} collective-permute-done((bf16[256,1024]{1,0:T(8,128)(2,1)S(1)}, bf16[256,1024]{1,0:T(8,128)(2,1)S(1)}, u32[]{:S(2)}, u32[]{:S(2)}) %collective-permute-start.9) | collective-permute-done | bytes 524320 | tf_op jit(solution)/shard_map/ppermute | solution.py:249
  52.6 2.8 %collective-permute-done.10.refs_4_ = bf16[256,1024]{1,0:T(8,128)(2,1)S(1)} collective-permute-done((bf16[256,1024]{1,0:T(8,128)(2,1)S(1)}, bf16[256,1024]{1,0:T(8,128)(2,1)S(1)}, u32[]{:S(2)}, u32[]{:S(2)}) %collective-permute-start.10) | collective-permute-done | bytes 524320 | tf_op jit(solution)/shard_map/ppermute | solution.py:249
  55.4 0.0 collective-permute-done.8.refs_2_
  55.4 0.0 collective-permute-start.17
  55.4 0.5 collective-permute-start.18
  55.9 0.0 collective-permute-start.19
  55.9 5.3 %shard_map.49 = (f32[256,3072]{1,0:T(8,128)S(1)}, f32[24,256,128]{2,1,0:T(8,128)S(1)}, f32[24,256,128]{2,1,0:T(8,128)S(1)}) custom-call(s32[3]{0:T(128)S(1)} %pad_add_fusion.ids, s32[64,128]{1,0:T(8,128)S(1)} %bitcast.6, bf16[256,3072]{1,0:T(8,128)(2,1)S(1)} %copy-done, f32[256,3072]{1,0:T(8,128)S(1)} %get-tuple-element.54.acc_in, ...), custom_call_target="tpu_custom_call", output_to_operand_aliasing={{1}: (4, {})} | custom-call | flops 3221225472 | bytes 3145728 | tf_op jit(solution)/shard_map/pallas_call | solution.py:212
  61.2 0.0 collective-permute-done.17.refs_2_
  61.2 0.0 collective-permute-done.18.refs_3_
  61.2 0.0 collective-permute-done.19.refs_4_
  61.2 6.0 %shard_map.50 = bf16[256,3072]{1,0:T(8,128)(2,1)} custom-call(s32[3]{0:T(128)S(1)} %pad_add_fusion.ids, s32[64,128]{1,0:T(8,128)S(1)} %bitcast.7, bf16[256,3072]{1,0:T(8,128)(2,1)S(1)} %copy-done, f32[256,3072]{1,0:T(8,128)S(1)} %get-tuple-element.60.acc_in, f32[24,256,128]{2,1,0:T(8,128)S(1)} %get-tuple-element.61.top_in, ...), custom_call_target="tpu_custom_call" | custom-call | flops 3221225472 | bytes 3145728 | tf_op jit(solution)/shard_map/pallas_call | solution.py:212
Async XLA Ops:
  0.0 24.0 %copy-start.3 = (s32[8192]{0:T(1024)S(1)}, s32[8192]{0:T(1024)}, u32[]{:S(2)}) copy-start(s32[8192]{0:T(1024)} %param.7) | copy-start | bytes 98308
  0.0 24.0 %copy-start = (bf16[256,3072]{1,0:T(8,128)(2,1)S(1)}, bf16[256,3072]{1,0:T(8,128)(2,1)}, u32[]{:S(2)}) copy-start(bf16[256,3072]{1,0:T(8,128)(2,1)} %q_ref.9) | copy-start | bytes 4718596
  0.0 2.1 %collective-permute-start = (bf16[256,1024]{1,0:T(8,128)(2,1)}, bf16[256,1024]{1,0:T(8,128)(2,1)S(1)}, u32[]{:S(2)}, u32[]{:S(2)}) collective-permute-start(bf16[256,1024]{1,0:T(8,128)(2,1)} %v_ref.1), channel_id=1, source_target_pairs={{0,1},{1,0},{2,3},{3,2},{4,5},{5,4},{6,7},{7,6},{8,9},{9,8},{10,11... | collective-permute-start | bytes 1572872 | tf_op jit(solution)/shard_map/ppermute | solution.py:249
  0.0 14.6 %collective-permute-start.2 = (bf16[256,1024]{1,0:T(8,128)(2,1)}, bf16[256,1024]{1,0:T(8,128)(2,1)S(1)}, u32[]{:S(2)}, u32[]{:S(2)}) collective-permute-start(bf16[256,1024]{1,0:T(8,128)(2,1)} %v_ref.1), channel_id=1, source_target_pairs={{0,2},{1,3},{2,0},{3,1},{4,6},{5,7},{6,4},{7,5},{8,10},{9,11},{10,... | collective-permute-start | bytes 1572872 | tf_op jit(solution)/shard_map/ppermute | solution.py:249
  1.6 14.3 %collective-permute-start.3 = (bf16[256,1024]{1,0:T(8,128)(2,1)}, bf16[256,1024]{1,0:T(8,128)(2,1)}, u32[]{:S(2)}, u32[]{:S(2)}) collective-permute-start(bf16[256,1024]{1,0:T(8,128)(2,1)} %v_ref.1), channel_id=1, source_target_pairs={{0,4},{1,5},{2,6},{3,7},{4,0},{5,1},{6,2},{7,3},{8,12},{9,13},{10,... | collective-permute-start | bytes 1572872 | tf_op jit(solution)/shard_map/ppermute | solution.py:249
  2.1 15.5 %collective-permute-start.4 = (bf16[256,1024]{1,0:T(8,128)(2,1)}, bf16[256,1024]{1,0:T(8,128)(2,1)}, u32[]{:S(2)}, u32[]{:S(2)}) collective-permute-start(bf16[256,1024]{1,0:T(8,128)(2,1)} %k_ref.1), channel_id=1, source_target_pairs={{0,1},{1,0},{2,3},{3,2},{4,5},{5,4},{6,7},{7,6},{8,9},{9,8},{10,11... | collective-permute-start | bytes 1572872 | tf_op jit(solution)/shard_map/ppermute | solution.py:249
  4.0 16.7 %collective-permute-start.1 = (bf16[256,1024]{1,0:T(8,128)(2,1)}, bf16[256,1024]{1,0:T(8,128)(2,1)S(1)}, u32[]{:S(2)}, u32[]{:S(2)}) collective-permute-start(bf16[256,1024]{1,0:T(8,128)(2,1)} %broadcast_select_fusion.3), channel_id=1, source_target_pairs={{0,8},{1,9},{2,10},{3,11},{4,12},{5,13},{6,14},{7,15},{8,16},{9,17... | collective-permute-start | bytes 1572872 | tf_op jit(solution)/shard_map/ppermute | solution.py:249
  5.6 18.4 %copy-start.1 = (bf16[256,1024]{1,0:T(8,128)(2,1)S(1)}, bf16[256,1024]{1,0:T(8,128)(2,1)}, u32[]{:S(2)}) copy-start(bf16[256,1024]{1,0:T(8,128)(2,1)} %k_ref.1) | copy-start | bytes 1572868
  5.6 18.4 %copy-start.2 = (bf16[256,1024]{1,0:T(8,128)(2,1)S(1)}, bf16[256,1024]{1,0:T(8,128)(2,1)}, u32[]{:S(2)}) copy-start(bf16[256,1024]{1,0:T(8,128)(2,1)} %v_ref.1) | copy-start | bytes 1572868
  15.9 15.7 %collective-permute-start.6 = (bf16[256,1024]{1,0:T(8,128)(2,1)S(1)}, bf16[256,1024]{1,0:T(8,128)(2,1)S(1)}, u32[]{:S(2)}, u32[]{:S(2)}) collective-permute-start(bf16[256,1024]{1,0:T(8,128)(2,1)S(1)} %broadcast_select_fusion.2), channel_id=1, source_target_pairs={{0,8},{1,9},{2,10},{3,11},{4,12},{5,13},{6,14},{7,15},{8,16},{9,17... | collective-permute-start | bytes 1572872 | tf_op jit(solution)/shard_map/ppermute | solution.py:249
  20.7 6.5 %collective-permute-start.7 = (bf16[256,1024]{1,0:T(8,128)(2,1)S(1)}, bf16[256,1024]{1,0:T(8,128)(2,1)S(1)}, u32[]{:S(2)}, u32[]{:S(2)}) collective-permute-start(bf16[256,1024]{1,0:T(8,128)(2,1)S(1)} %collective-permute-done.1.refs_3_.refs_0_), channel_id=1, source_target_pairs={{0,1},{1,0},{2,3},{3,2},{4,5},{5,4},{6,7},{7,6},{8,9},{9,8},{10,11... | collective-permute-start | bytes 1572872 | tf_op jit(solution)/shard_map/ppermute | solution.py:249
  21.9 14.4 %collective-permute-start.5 = (bf16[256,1024]{1,0:T(8,128)(2,1)S(1)}, bf16[256,1024]{1,0:T(8,128)(2,1)S(1)}, u32[]{:S(2)}, u32[]{:S(2)}) collective-permute-start(bf16[256,1024]{1,0:T(8,128)(2,1)S(1)} %get-tuple-element.64), channel_id=1, source_target_pairs={{0,4},{1,5},{2,6},{3,7},{4,0},{5,1},{6,2},{7,3},{8,12},{9,13},{10,... | collective-permute-start | bytes 1572872 | tf_op jit(solution)/shard_map/ppermute | solution.py:249
  22.3 14.5 %collective-permute-start.11 = (bf16[256,1024]{1,0:T(8,128)(2,1)S(1)}, bf16[256,1024]{1,0:T(8,128)(2,1)S(1)}, u32[]{:S(2)}, u32[]{:S(2)}) collective-permute-start(bf16[256,1024]{1,0:T(8,128)(2,1)S(1)} %get-tuple-element.63), channel_id=1, source_target_pairs={{0,2},{1,3},{2,0},{3,1},{4,6},{5,7},{6,4},{7,5},{8,10},{9,11},{10,... | collective-permute-start | bytes 1572872 | tf_op jit(solution)/shard_map/ppermute | solution.py:249
  27.2 9.8 %collective-permute-start.12 = (bf16[256,1024]{1,0:T(8,128)(2,1)S(1)}, bf16[256,1024]{1,0:T(8,128)(2,1)S(1)}, u32[]{:S(2)}, u32[]{:S(2)}) collective-permute-start(bf16[256,1024]{1,0:T(8,128)(2,1)S(1)} %collective-permute-done.2.refs_0_), channel_id=1, source_target_pairs={{0,1},{1,0},{2,3},{3,2},{4,5},{5,4},{6,7},{7,6},{8,9},{9,8},{10,11... | collective-permute-start | bytes 1572872 | tf_op jit(solution)/shard_map/ppermute | solution.py:249
  27.2 11.3 %collective-permute-start.13 = (bf16[256,1024]{1,0:T(8,128)(2,1)}, bf16[256,1024]{1,0:T(8,128)(2,1)S(1)}, u32[]{:S(2)}, u32[]{:S(2)}) collective-permute-start(bf16[256,1024]{1,0:T(8,128)(2,1)} %collective-permute-done.3.refs_1_), channel_id=1, source_target_pairs={{0,1},{1,0},{2,3},{3,2},{4,5},{5,4},{6,7},{7,6},{8,9},{9,8},{10,11... | collective-permute-start | bytes 1572872 | tf_op jit(solution)/shard_map/ppermute | solution.py:249
  36.3 3.5 %collective-permute-start.15 = (bf16[256,1024]{1,0:T(8,128)(2,1)S(1)}, bf16[256,1024]{1,0:T(8,128)(2,1)S(1)}, u32[]{:S(2)}, u32[]{:S(2)}) collective-permute-start(bf16[256,1024]{1,0:T(8,128)(2,1)S(1)} %collective-permute-done.5.refs_3_.refs_1_), channel_id=1, source_target_pairs={{0,1},{1,0},{2,3},{3,2},{4,5},{5,4},{6,7},{7,6},{8,9},{9,8},{10,11... | collective-permute-start | bytes 1572872 | tf_op jit(solution)/shard_map/ppermute | solution.py:249
  36.3 3.5 %collective-permute-start.16 = (bf16[256,1024]{1,0:T(8,128)(2,1)S(1)}, bf16[256,1024]{1,0:T(8,128)(2,1)S(1)}, u32[]{:S(2)}, u32[]{:S(2)}) collective-permute-start(bf16[256,1024]{1,0:T(8,128)(2,1)S(1)} %collective-permute-done.6.refs_4_), channel_id=1, source_target_pairs={{0,1},{1,0},{2,3},{3,2},{4,5},{5,4},{6,7},{7,6},{8,9},{9,8},{10,11... | collective-permute-start | bytes 1572872 | tf_op jit(solution)/shard_map/ppermute | solution.py:249
  36.8 3.0 %collective-permute-start.14 = (bf16[256,1024]{1,0:T(8,128)(2,1)S(1)}, bf16[256,1024]{1,0:T(8,128)(2,1)S(1)}, u32[]{:S(2)}, u32[]{:S(2)}) collective-permute-start(bf16[256,1024]{1,0:T(8,128)(2,1)S(1)} %collective-permute-done.11.refs_2_), channel_id=1, source_target_pairs={{0,1},{1,0},{2,3},{3,2},{4,5},{5,4},{6,7},{7,6},{8,9},{9,8},{10,11... | collective-permute-start | bytes 1572872 | tf_op jit(solution)/shard_map/ppermute | solution.py:249
  36.9 18.4 %collective-permute-start.8 = (bf16[256,1024]{1,0:T(8,128)(2,1)S(1)}, bf16[256,1024]{1,0:T(8,128)(2,1)S(1)}, u32[]{:S(2)}, u32[]{:S(2)}) collective-permute-start(bf16[256,1024]{1,0:T(8,128)(2,1)S(1)} %collective-permute-done.5.refs_3_.refs_1_), channel_id=1, source_target_pairs={{0,2},{1,3},{2,0},{3,1},{4,6},{5,7},{6,4},{7,5},{8,10},{9,11},{10,... | collective-permute-start | bytes 1572872 | tf_op jit(solution)/shard_map/ppermute | solution.py:249
  38.5 14.1 %collective-permute-start.9 = (bf16[256,1024]{1,0:T(8,128)(2,1)S(1)}, bf16[256,1024]{1,0:T(8,128)(2,1)S(1)}, u32[]{:S(2)}, u32[]{:S(2)}) collective-permute-start(bf16[256,1024]{1,0:T(8,128)(2,1)S(1)} %broadcast_select_fusion.4), channel_id=1, source_target_pairs={{0,4},{1,5},{2,6},{3,7},{4,0},{5,1},{6,2},{7,3},{8,12},{9,13},{10,... | collective-permute-start | bytes 1572872 | tf_op jit(solution)/shard_map/ppermute | solution.py:249
  39.8 15.6 %collective-permute-start.10 = (bf16[256,1024]{1,0:T(8,128)(2,1)S(1)}, bf16[256,1024]{1,0:T(8,128)(2,1)S(1)}, u32[]{:S(2)}, u32[]{:S(2)}) collective-permute-start(bf16[256,1024]{1,0:T(8,128)(2,1)S(1)} %broadcast_select_fusion.1), channel_id=1, source_target_pairs={{0,8},{1,9},{2,10},{3,11},{4,12},{5,13},{6,14},{7,15},{8,16},{9,17... | collective-permute-start | bytes 1572872 | tf_op jit(solution)/shard_map/ppermute | solution.py:249
  55.4 5.8 %collective-permute-start.17 = (bf16[256,1024]{1,0:T(8,128)(2,1)S(1)}, bf16[256,1024]{1,0:T(8,128)(2,1)S(1)}, u32[]{:S(2)}, u32[]{:S(2)}) collective-permute-start(bf16[256,1024]{1,0:T(8,128)(2,1)S(1)} %collective-permute-done.8.refs_2_), channel_id=1, source_target_pairs={{0,1},{1,0},{2,3},{3,2},{4,5},{5,4},{6,7},{7,6},{8,9},{9,8},{10,11... | collective-permute-start | bytes 1572872 | tf_op jit(solution)/shard_map/ppermute | solution.py:249
  55.4 5.8 %collective-permute-start.18 = (bf16[256,1024]{1,0:T(8,128)(2,1)S(1)}, bf16[256,1024]{1,0:T(8,128)(2,1)S(1)}, u32[]{:S(2)}, u32[]{:S(2)}) collective-permute-start(bf16[256,1024]{1,0:T(8,128)(2,1)S(1)} %collective-permute-done.9.refs_3_), channel_id=1, source_target_pairs={{0,1},{1,0},{2,3},{3,2},{4,5},{5,4},{6,7},{7,6},{8,9},{9,8},{10,11... | collective-permute-start | bytes 1572872 | tf_op jit(solution)/shard_map/ppermute | solution.py:249
  55.9 5.3 %collective-permute-start.19 = (bf16[256,1024]{1,0:T(8,128)(2,1)S(1)}, bf16[256,1024]{1,0:T(8,128)(2,1)S(1)}, u32[]{:S(2)}, u32[]{:S(2)}) collective-permute-start(bf16[256,1024]{1,0:T(8,128)(2,1)S(1)} %collective-permute-done.10.refs_4_), channel_id=1, source_target_pairs={{0,1},{1,0},{2,3},{3,2},{4,5},{5,4},{6,7},{7,6},{8,9},{9,8},{10,11... | collective-permute-start | bytes 1572872 | tf_op jit(solution)/shard_map/ppermute | solution.py:249
